TPU v7x, 256 devices: a whole 4x4x8 slice. The times are simulated.
256 devices in a mesh: pair: 32 (over z, y), occ: 8 (over x, core).
Axes of the slice: x: 4, y: 4, z: 8, core: 2. Of those that a mesh axis runs over, the one named last changes fastest.
Arguments:
- amplitudes: float32 [256, 128, 128], P('pair'), may hold values from -4 to 4
- exchange_ints: float32 [256, 128, 128], P('pair'), may hold values from -6 to 6
- pno_energy: float32 [256, 128], P('pair'), may hold values from 0.3 to 3
- pair_shift: float32 [256], P('pair'), may hold values from 0.5 to 2
- coefficients: bfloat16 [256, 512, 128], P('pair'), may hold values from -0.5 to 0.5
- domain_tiles: int32 [256, 4], P('pair'), may hold values from 0 to 3, each once within a row
- couple_owner: int32 [8, 256, 8, 1], P('occ', 'pair'), may hold values from 0 to 31; in each aligned block of 64 rows (0 to 63, 64 to 127, ..., all dimensions but the last counted through in order) at most 3 rows name the same one
- couple_index: int32 [8, 256, 8], P('occ', 'pair'), may hold values from 0 to 7
- couple_weight: float32 [8, 256, 8], P('occ', 'pair'), may hold values from -0.5 to 0.5
Outputs:
- final_amplitudes: float32 [256, 128, 128], P('pair')
- final_residual: float32 [256, 128, 128], P('pair')
Inputs may be any that keep to these rules, and one draw needn't show every extreme that they name: `couple_owner`: among the couplings held by one device (one block of 64 entries), no owner is named more than 3 times. `domain_tiles`: the tiles of one pair's domain are distinct.
All inputs are finite; a program needn't handle non-finite values.
Results may differ from a plain program's by a relative error of at most 0.0003.
Values may be sent and summed in bfloat16 or wider, within the bound.
A program may use at most 128 MiB of HBM per device.

v0:
```python
import jax
import jax.numpy as jnp
from jax import lax
from jax.sharding import Mesh
from jax.sharding import PartitionSpec as P

ITERS = 2
PAIR = ("pair_0", "pair_1")


HIGHEST = lax.Precision.HIGHEST


def in_blocks(x, dim, peers):
    before, after = (x.shape[:dim], x.shape[dim + 1 :])
    return jnp.moveaxis(x.reshape(*before, peers, -1, *after), dim, 0)


def joined_along(pieces, dim):
    lengths = list(pieces.shape[1:])
    lengths[dim] *= pieces.shape[0]
    return jnp.moveaxis(pieces, 0, dim).reshape(lengths)


def moved_by_axis(pieces, axes, order):
    lengths = [lax.axis_size(a) for a in axes]
    pieces = pieces.reshape(*lengths, *pieces.shape[1:])
    for k in order:
        pieces = lax.all_to_all(pieces, axes[k], split_axis=k, concat_axis=k, tiled=True)
    return pieces.reshape(-1, *pieces.shape[len(axes) :])


def stepwise_exchange(x, axes, order, split_dim, concat_dim):
    pieces = in_blocks(x, split_dim, lax.axis_size(axes))
    return joined_along(moved_by_axis(pieces, axes, order), concat_dim)


def over_pieces(x, axis):
    pieces = lax.all_gather(x, axis)
    return pieces.sum(axis=0)


def local(
    amplitudes,
    exchange_ints,
    pno_energy,
    pair_shift,
    coefficients,
    domain_tiles,
    couple_owner,
    couple_index,
    couple_weight,
):
    pair_count = amplitudes.shape[0]
    pno_width = amplitudes.shape[1]
    domain = coefficients.shape[1]
    tile_count = domain_tiles.shape[1]
    couple_count = couple_index.shape[2]
    peer_count = lax.axis_size(PAIR)
    owners = couple_owner.reshape(-1)
    local_index = couple_index.reshape(-1)
    weights = couple_weight.reshape(pair_count, couple_count)
    total_count = owners.shape[0]
    capacity = max(2, 3 * total_count // (2 * peer_count))
    slot_total = peer_count * capacity
    position = jnp.arange(total_count, dtype=jnp.int32)
    same_owner = (owners[:, None] == owners[None, :]) & (position[None, :] < position[:, None])
    slot_rank = jnp.sum(same_owner.astype(jnp.int32), axis=1)
    slot_ids = owners * capacity + slot_rank
    requester_tiles = jnp.repeat(domain_tiles, couple_count, axis=0)
    payload = jnp.concatenate([local_index[:, None], requester_tiles], axis=1)
    requests = jnp.full((slot_total, 1 + tile_count), -1, jnp.int32).at[slot_ids].set(payload)
    arrived = stepwise_exchange(requests, PAIR, (0, 1), 0, 0)
    wanted = arrived[:, 0]
    their_tiles = arrived[:, 1:]
    pick_pair = wanted[:, None] == jnp.arange(pair_count, dtype=jnp.int32)[None, :]
    tile_match = their_tiles[:, :, None, None] == domain_tiles[None, None, :, :]
    selector = (pick_pair[:, None, :, None] & tile_match).astype(jnp.bfloat16)
    selector = selector.reshape(slot_total * tile_count, pair_count * tile_count)
    tile_blocks = coefficients.reshape(pair_count * tile_count, domain // tile_count * pno_width)
    moved_tiles = jnp.dot(selector, tile_blocks, preferred_element_type=jnp.float32).astype(
        jnp.bfloat16
    )
    moved_tiles = moved_tiles.reshape(slot_total, domain, pno_width)
    returned = lax.all_to_all(moved_tiles, PAIR, split_axis=0, concat_axis=0, tiled=True)
    their_coef = jnp.take(returned, slot_ids, axis=0).reshape(
        pair_count, couple_count, domain, pno_width
    )
    intersection = jnp.einsum(
        "pfa,pcfb->pcab", coefficients, their_coef, preferred_element_type=jnp.float32
    )
    denominator = pno_energy[:, :, None] + pno_energy[:, None, :] + pair_shift[:, None, None]
    global_ids = owners * pair_count + local_index
    current = amplitudes
    residual = amplitudes
    for iteration in range(ITERS):
        all_amps = lax.all_gather(current, PAIR, axis=0, tiled=True)
        partner_amp = jnp.take(all_amps, global_ids, axis=0)
        partner_amp = partner_amp.reshape(pair_count, couple_count, pno_width, pno_width)
        inner_prod = jnp.einsum("pcab,pcbd->pcad", intersection, partner_amp, precision=HIGHEST)
        outer_prod = jnp.einsum("pcad,pced->pcae", inner_prod, intersection, precision=HIGHEST)
        partial_value = jnp.einsum("pc,pcae->pae", weights, outer_prod, precision=HIGHEST)
        coupled = over_pieces(partial_value, "occ")
        residual = exchange_ints + denominator * current - coupled
        current = current - residual / denominator
    return (current, residual)


def solution(mesh):
    split = Mesh(mesh.devices.reshape(8, 4, mesh.shape["occ"]), ("pair_0", "pair_1", "occ"))
    in_specs = (
        P(PAIR, None, None),
        P(PAIR, None, None),
        P(PAIR, None),
        P(PAIR),
        P(PAIR, None, None),
        P(PAIR, None),
        P("occ", PAIR, None, None),
        P("occ", PAIR, None),
        P("occ", PAIR, None),
    )
    out_specs = (P(PAIR, None, None), P(PAIR, None, None))
    return jax.shard_map(local, mesh=split, in_specs=in_specs, out_specs=out_specs, check_vma=False)
```

profile of v0, /device:TPU:1, one launch (start us, length us, event | category | flops | bytes accessed | tf_op | source)
XLA Modules:
  0.0 751.8 jit_solution(6762921172561022608)
XLA Ops:
  7.2 0.0 copy-start
  7.2 0.0 all-gather.7.cloned.1.call-start
  7.2 0.7 all-gather.7.cloned.1.call-update
  7.9 0.5 broadcast.128
  8.4 1.3 reduce.3
  9.8 0.1 reshape.162
  9.9 0.7 broadcast_multiply_fusion
  10.5 0.1 mul.38
  10.6 0.8 broadcast_in_dim.37
  11.4 0.1 reshape.163
  11.5 0.8 broadcast_in_dim_reshape.2
  12.2 0.1 copy.34
  12.3 0.2 convert_reduce_fusion
  12.5 0.7 scatter_custom_fusion
  13.3 15.9 %all_to_all.15 = s32[8,4,3,5]{3,1,2,0:T(4,128)S(1)} all-to-all(s32[8,4,3,5]{3,1,2,0:T(4,128)S(1)} %copy.36), channel_id=1, replica_groups=mesh['pair_0'=8,'pair_1'=4,'occ'=8] {'pair_0'}, dimensions={0} | all-to-all | bytes 3840 | tf_op jit(solution)/shard_map/all_to_all | solution.py:29
  29.2 0.8 copy.37
  30.0 4.2 all-to-all-start.1
  34.2 0.8 copy.40
  34.9 1.5 reshape.164
  36.5 2.3 all-to-all-done.1
  38.8 0.2 copy.38
  39.0 0.1 reshape_reshape.7
  39.1 0.1 copy.39
  39.3 0.3 compare_and_fusion
  39.6 1.3 and.37
  40.9 6.4 convolution_convert_fusion
  47.3 19.6 %reshape.165 = bf16[96,512,128]{2,1,0:T(8,128)(2,1)} reshape(bf16[384,16384]{1,0:T(8,128)(2,1)} %convolution_convert_fusion) | data formatting | bytes 25165824 | tf_op jit(solution)/shard_map/reshape | solution.py:84
  66.9 5.2 all-to-all-start.2
  72.2 0.0 all-gather.11.cloned.1.call-start
  72.2 0.1 reduce_sum.32
  72.3 0.1 reshape.166
  72.4 351.0 %all-to-all-done.2 = bf16[96,512,128]{2,1,0:T(8,128)(2,1)} async-done(((bf16[96,512,128]{2,1,0:T(8,128)(2,1)}), bf16[96,512,128]{2,1,0:T(8,128)(2,1)}, u32[]{:S(2)}, u32[]{:S(2)}) %all-to-all-start.2) | async-done | bytes 12582944 | tf_op jit(solution)/shard_map/all_to_all | solution.py:85
  423.4 10.2 %gather_fusion = bf16[64,512,128]{2,1,0:T(8,128)(2,1)} fusion(bf16[96,512,128]{2,1,0:T(8,128)(2,1)} %all-to-all-done.2, s32[1024]{0:T(1024)S(1)} %pad_clamp_fusion.1), kind=kCustom, calls=%fused_computation.2 | custom fusion | bytes 16777472 | tf_op jit(solution)/shard_map/jit(_take)/gather | solution.py:86
  433.6 12.2 %copy.41 = bf16[64,512,128]{1,2,0:T(8,128)(2,1)} copy(bf16[64,512,128]{2,1,0:T(8,128)(2,1)} %gather_fusion) | data formatting | bytes 16777216 | tf_op jit(solution)/shard_map/jit(_take)/gather | solution.py:86
  445.8 7.7 %fusion = f32[8,8,128,128]{3,2,1,0:T(8,128)} fusion(bf16[8,8,512,128]{2,3,1,0:T(8,128)(2,1)} %bitcast.63, pred[8,8]{1,0:T(8,128)(4,1)S(1)} %compare_and_fusion.1, bf16[8,512,128]{2,1,0:T(8,128)(2,1)S(1)} %copy-done.6), kind=kOutput, calls=%fused_computation.5 | convolution fusion | flops 1077936128 | bytes 13631552 | tf_op jit(solution)/shard_map/pfa,pcfb->pcab/dot_general | solution.py:89
  453.6 8.5 %gather_fusion.1 = f32[64,128,128]{2,1,0:T(8,128)} fusion(f32[256,128,128]{2,1,0:T(8,128)} %all-gather.7.cloned.1.call-done, s32[1024]{0:T(1024)S(1)} %pad_clamp_fusion), kind=kCustom, calls=%fused_computation.clone | custom fusion | bytes 8388864 | tf_op jit(solution)/shard_map/jit(_take)/gather | solution.py:98
  462.1 2.7 broadcast_select_fusion.1
  464.8 0.8 copy-done.1
  465.6 7.3 fusion.14
  472.9 5.8 fusion.15
  478.7 0.0 copy-start.4
  478.7 0.0 copy-start.5
  478.7 0.0 copy-start.7
  478.7 0.0 copy-start.10
  478.8 6.1 fusion.5
  484.8 0.0 all-gather.11.cloned.1.call-update
  484.9 0.0 all-gather.9.cloned.1.call-start
  484.9 48.7 %all-gather.11.cloned.1.call-done = f32[64,128,128]{2,1,0:T(8,128)} async-done(((f32[8,128,128]{2,1,0:T(8,128)}), f32[64,128,128]{2,1,0:T(8,128)}) %all-gather.11.cloned.1.call-update) | async-done | bytes 4194320 | tf_op jit(solution)/shard_map/all_gather | solution.py:39
  533.6 2.5 reduce_sum.34
  536.1 1.0 divide_subtract_fusion.1
  537.2 0.0 all-gather.9.cloned.1.call-update
  537.2 0.0 all-gather.13.cloned.1.call-start
  537.2 139.9 %all-gather.9.cloned.1.call-done = f32[256,128,128]{2,1,0:T(8,128)} async-done(((f32[8,128,128]{2,1,0:T(8,128)}), f32[256,128,128]{2,1,0:T(8,128)}) %all-gather.9.cloned.1.call-update) | async-done | bytes 16777232 | tf_op jit(solution)/shard_map/all_gather | solution.py:97
  677.2 8.5 %gather_fusion.2 = f32[64,128,128]{2,1,0:T(8,128)} fusion(f32[256,128,128]{2,1,0:T(8,128)} %all-gather.9.cloned.1.call-done, s32[1024]{0:T(1024)S(1)} %pad_clamp_fusion), kind=kCustom, calls=%fused_computation.1.clone | custom fusion | bytes 8388864 | tf_op jit(solution)/shard_map/jit(_take)/gather | solution.py:98
  685.7 2.7 broadcast_select_fusion
  688.4 0.8 copy-done.2
  689.1 7.3 fusion.16
  696.4 5.9 fusion.17
  702.3 0.0 copy-start.3
  702.3 6.1 fusion.3
  708.4 0.0 all-gather.13.cloned.1.call-update
  708.4 32.6 %all-gather.13.cloned.1.call-done = f32[64,128,128]{2,1,0:T(8,128)} async-done(((f32[8,128,128]{2,1,0:T(8,128)}), f32[64,128,128]{2,1,0:T(8,128)}) %all-gather.13.cloned.1.call-update) | async-done | bytes 4194320 | tf_op jit(solution)/shard_map/all_gather | solution.py:39
  741.1 2.5 reduce_sum.35
  743.6 1.2 divide_subtract_fusion
  (26 shorter events, 0.1 us)
Async XLA Ops:
  7.2 471.5 %copy-start = (f32[1,8,8]{2,1,0:T(8,128)S(1)}, f32[1,8,8]{2,1,0:T(8,128)}, u32[]{:S(2)}) copy-start(f32[1,8,8]{2,1,0:T(8,128)} %param.19) | copy-start | bytes 772
  7.2 446.4 %all-gather.7.cloned.1.call-start = ((), (), s32[]{:S(2)}) async-start(), calls=%async_computation.3 | async-start | bytes 17301504 | tf_op jit(solution)/shard_map/all_gather | solution.py:97
  30.0 8.8 %all-to-all-start.1 = ((s32[8,4,3,5]{0,2,3,1:T(4,128)}), s32[8,4,3,5]{0,2,3,1:T(4,128)S(1)}, u32[]{:S(2)}, u32[]{:S(2)}) async-start(s32[8,4,3,5]{0,2,3,1:T(4,128)} %copy.37), calls=%async_computation.1 | async-start | bytes 81920 | tf_op jit(solution)/shard_map/all_to_all | solution.py:29
  66.9 5.4 copy-start.9
  66.9 5.5 copy-start.8
  66.9 356.5 %all-to-all-start.2 = ((bf16[96,512,128]{2,1,0:T(8,128)(2,1)}), bf16[96,512,128]{2,1,0:T(8,128)(2,1)}, u32[]{:S(2)}, u32[]{:S(2)}) async-start(bf16[96,512,128]{2,1,0:T(8,128)(2,1)} %reshape.165), calls=%async_computation.2 | async-start | bytes 25165824 | tf_op jit(solution)/shard_map/all_to_all | solution.py:85
  72.2 461.4 %all-gather.11.cloned.1.call-start = ((), (), s32[]{:S(2)}) async-start(), calls=%async_computation.5 | async-start | bytes 4718592 | tf_op jit(solution)/shard_map/all_gather | solution.py:39
  433.6 12.2 %copy-start.6 = (bf16[8,512,128]{2,1,0:T(8,128)(2,1)S(1)}, bf16[8,512,128]{2,1,0:T(8,128)(2,1)}, u32[]{:S(2)}) copy-start(bf16[8,512,128]{2,1,0:T(8,128)(2,1)} %param.15) | copy-start | bytes 3145732
  462.1 3.4 copy-start.1
  478.7 57.4 %copy-start.4 = (f32[8,128,128]{2,1,0:T(8,128)S(1)}, f32[8,128,128]{2,1,0:T(8,128)}, u32[]{:S(2)}) copy-start(f32[8,128,128]{2,1,0:T(8,128)} %param.11) | copy-start | bytes 1572868
  478.7 57.4 %copy-start.5 = (f32[8,128,128]{2,1,0:T(8,128)S(1)}, f32[8,128,128]{2,1,0:T(8,128)}, u32[]{:S(2)}) copy-start(f32[8,128,128]{2,1,0:T(8,128)} %param.12) | copy-start | bytes 1572868
  478.7 57.4 %copy-start.7 = (f32[8,128]{1,0:T(8,128)S(1)}, f32[8,128]{1,0:T(8,128)}, u32[]{:S(2)}) copy-start(f32[8,128]{1,0:T(8,128)} %param.13) | copy-start | bytes 12292
  478.7 57.4 %copy-start.10 = (f32[8]{0:T(128)S(1)}, f32[8]{0:T(128)}, u32[]{:S(2)}) copy-start(f32[8]{0:T(128)} %param.14) | copy-start | bytes 100
  484.9 192.3 %all-gather.9.cloned.1.call-start = ((), (), s32[]{:S(2)}) async-start(), calls=%async_computation.4 | async-start | bytes 17301504 | tf_op jit(solution)/shard_map/all_gather | solution.py:97
  537.2 203.9 %all-gather.13.cloned.1.call-start = ((), (), s32[]{:S(2)}) async-start(), calls=%async_computation.6 | async-start | bytes 4718592 | tf_op jit(solution)/shard_map/all_gather | solution.py:39
  685.7 3.4 copy-start.2
  702.3 41.3 %copy-start.3 = (f32[8,128,128]{2,1,0:T(8,128)S(1)}, f32[8,128,128]{2,1,0:T(8,128)}, u32[]{:S(2)}) copy-start(f32[8,128,128]{2,1,0:T(8,128)} %divide_subtract_fusion.1) | copy-start | bytes 1572868
Sparse Core Ops, SparseCore 0:
  10.6 325.4 all-gather.6
  485.0 48.5 all-gather.10
  537.3 139.8 all-gather.8
  708.6 32.4 all-gather.12
where the time goes:
time: 758 us; the launch traced here: 752 us
  waiting for transfers between devices  575 us (76%)
  local copies, waits for them, and re-layouts  68.8 us (9%)
  matrix products  52.6 us (7%)
  blocking collectives  15.9 us (2%)
  other arithmetic  15.2 us (2%)
  between operations  14.5 us (2%)
  starting transfers between devices  9.56 us (1%)
    all_to_all x1, waiting for transfers between devices, local(): lax.all_to_all(moved_tiles, PAIR, split_axis=0, concat_axis=0, tiled=True)  351 us
    all_gather x2, waiting for transfers between devices, local(): all_amps = lax.all_gather(current, PAIR, axis=0, tiled=True)  140 us
    all_gather x2, waiting for transfers between devices, over_pieces(): pieces = lax.all_gather(x, axis)  81.3 us
    gather x2, local copies, waits for them, and re-layouts, local(): jnp.take(returned, slot_ids, axis=0)  22.4 us
    reshape x1, local copies, waits for them, and re-layouts, local(): moved_tiles = moved_tiles.reshape(slot_total, domain, pno_width)  19.6 us
    gather x2, local copies, waits for them, and re-layouts, local(): partner_amp = jnp.take(all_amps, global_ids, axis=0)  17.1 us
    all_to_all x1, blocking collectives, moved_by_axis(): lax.all_to_all(pieces, axes[k], split_axis=k, concat_axis=k, tiled=True)  15.9 us
  transfers between devices with their start and end apart: 6, of which 5 were waited for; matrix products, arithmetic and copies ran while one was open for 9% of the time, Pallas kernels for 0%

commit v1 on v0

v1 whole, which is shorter than its diff:
```python
import jax
import jax.numpy as jnp
from jax import lax
from jax.sharding import Mesh
from jax.sharding import PartitionSpec as P

ITERS = 2
PAIR = ("pair_0", "pair_1")


def local(
    amplitudes,
    exchange_ints,
    pno_energy,
    pair_shift,
    coefficients,
    domain_tiles,
    couple_owner,
    couple_index,
    couple_weight,
):
    pairs, tiles = domain_tiles.shape
    width = amplitudes.shape[1]
    owners = couple_owner[0, :, :, 0]
    places = couple_index[0]
    weights = couple_weight[0]
    me = lax.axis_index("occ")
    peers = lax.axis_size(PAIR)
    blocks = coefficients.reshape(pairs, tiles, -1, width)
    match = domain_tiles[:, None, :] == jnp.arange(tiles, dtype=jnp.int32)[None, :, None]
    ordered = jnp.sum(
        jnp.where(match[..., None, None], blocks[:, None], jnp.zeros((), blocks.dtype)),
        axis=2,
        dtype=blocks.dtype,
    ).reshape(coefficients.shape)
    own = lax.dynamic_index_in_dim(ordered, me, 0, keepdims=False)
    theirs = lax.all_gather(own, PAIR)
    named = (owners[:, :, None] == jnp.arange(peers, dtype=jnp.int32)) * weights[:, :, None]
    place = places[:, :, None] == jnp.arange(pairs, dtype=jnp.int32)
    table = jnp.sum(named[:, :, None, :] * place[:, :, :, None], axis=1)
    table = lax.psum_scatter(table, "occ", scatter_dimension=1, tiled=True)[:, 0]
    overlap = jnp.einsum("pfa,qfb->pqab", ordered, theirs, preferred_element_type=jnp.float32)
    pick = lambda x: lax.dynamic_index_in_dim(x, me, 0, keepdims=False)
    energy, shift = pick(pno_energy), pick(pair_shift)
    denominator = energy[:, None] + energy[None, :] + shift
    current, exchange = pick(amplitudes), pick(exchange_ints)
    residual = current
    for _ in range(ITERS):
        amps = lax.all_gather(current, PAIR)
        inner = jnp.einsum("pqab,qbd->pqad", overlap, amps, precision=lax.Precision.HIGH)
        inner = inner * table[:, :, None, None]
        part = jnp.einsum("pqad,pqed->pae", inner, overlap, precision=lax.Precision.HIGH)
        coupled = lax.psum_scatter(part, "occ", scatter_dimension=0, tiled=True)[0]
        residual = exchange + denominator * current - coupled
        current = current - residual / denominator
    return lax.all_gather(current, "occ"), lax.all_gather(residual, "occ")


def solution(mesh):
    split = Mesh(mesh.devices.reshape(8, 4, mesh.shape["occ"]), ("pair_0", "pair_1", "occ"))
    in_specs = (
        P(PAIR, None, None),
        P(PAIR, None, None),
        P(PAIR, None),
        P(PAIR),
        P(PAIR, None, None),
        P(PAIR, None),
        P("occ", PAIR, None, None),
        P("occ", PAIR, None),
        P("occ", PAIR, None),
    )
    out_specs = (P(PAIR, None, None), P(PAIR, None, None))
    return jax.shard_map(local, mesh=split, in_specs=in_specs, out_specs=out_specs, check_vma=False)
```

time: 758 us -> 427 us (0.56)
  waiting for transfers between devices: 575 us -> 261 us
  local copies, waits for them, and re-layouts: 68.8 us -> 7 us
  blocking collectives: 15.9 us -> 52.7 us
  matrix products: 52.6 us -> 82.9 us
  starting transfers between devices: 9.56 us -> 0.21 us
    all_to_all x2 -> x0, waiting for transfers between devices: 353 us -> none  [the longest x1 351 us: local(): lax.all_to_all(moved_tiles, PAIR, split_axis=0, concat_axis=0, tiled=True)]
    reduce_scatter x0 -> x2, waiting for transfers between devices: none -> 64 us  [local(): coupled = lax.psum_scatter(part, 'occ', scatter_dimension=0, tiled=True)[0]]
    gather x4 -> x0, local copies, waits for them, and re-layouts: 39.5 us -> none  [the longest x2 22.4 us: local(): jnp.take(returned, slot_ids, axis=0)]
    dot_general x8 -> x5, matrix products: 52.6 us -> 82.9 us  [the longest x2 42 us: local(): jnp.einsum('pqad,pqed->pae', inner, overlap, precision=lax.Precision.HIGH)]
    all_gather x0 -> x2, blocking collectives: none -> 29 us  [local(): return (lax.all_gather(current, 'occ'), lax.all_gather(residual, 'occ'))]
    all_gather x4 -> x3, waiting for transfers between devices: 221 us -> 197 us  [the longest x2 143 us: local(): amps = lax.all_gather(current, PAIR)]
    unnamed x0 -> x1, blocking collectives: none -> 23.7 us
    reshape x5 -> x0, local copies, waits for them, and re-layouts: 21.3 us -> none  [the longest x1 19.6 us: local(): moved_tiles = moved_tiles.reshape(slot_total, domain, pno_width)]
  transfers between devices with their start and end apart: 6 -> 5, of which waited for: 5 -> 5; matrix products, arithmetic and copies ran while one was open for 9% -> 4% of each run, Pallas kernels for 0% -> 0%
where the time goes in v1:
time: 427 us
  waiting for transfers between devices  261 us (61%)
  matrix products  82.9 us (19%)
  blocking collectives  52.7 us (12%)
  between operations  13.9 us (3%)
  other arithmetic  8.49 us (2%)
  local copies, waits for them, and re-layouts  7 us (2%)
    all_gather x2, waiting for transfers between devices, local(): amps = lax.all_gather(current, PAIR)  143 us
    reduce_scatter x2, waiting for transfers between devices, local(): coupled = lax.psum_scatter(part, 'occ', scatter_dimension=0, tiled=True)[0]  64 us
    all_gather x1, waiting for transfers between devices, local(): theirs = lax.all_gather(own, PAIR)  54.3 us
    dot_general x2, matrix products, local(): jnp.einsum('pqad,pqed->pae', inner, overlap, precision=lax.Precision.HIGH)  42 us
    dot_general x2, matrix products, local(): jnp.einsum('pqab,qbd->pqad', overlap, amps, precision=lax.Precision.HIGH)  30.6 us
    all_gather x2, blocking collectives, local(): return (lax.all_gather(current, 'occ'), lax.all_gather(residual, 'occ'))  29 us
    unnamed x1, blocking collectives  23.7 us
    dot_general x1, matrix products, local(): jnp.einsum('pfa,qfb->pqab', ordered, theirs, preferred_element_type=jnp.f...  10.3 us
  transfers between devices with their start and end apart: 5, of which 5 were waited for; matrix products, arithmetic and copies ran while one was open for 4% of the time, Pallas kernels for 0%

profile of v1, /device:TPU:1, one launch (start us, length us, event | category | flops | bytes accessed | tf_op | source)
XLA Modules:
  0.0 426.6 jit_solution(17551176442349887302)
XLA Ops:
  7.2 0.0 copy-start
  7.2 0.0 all-gather.6.cloned.1.call-start
  7.2 0.8 copy.19
  8.0 2.8 select_reduce_fusion
  10.8 0.7 constant_dynamic-slice_fusion
  11.5 0.0 all-gather.6.cloned.1.call-update
  11.5 0.0 all-gather.4.cloned.1.call-start
  11.6 1.5 constant_dynamic-slice_fusion.2
  13.1 0.0 all-gather.4.cloned.1.call-update
  13.1 0.0 reduce-scatter.3.cloned.1.call-start
  13.1 0.8 fusion.20
  13.9 0.8 fusion.19
  14.7 0.1 multiply_reduce_fusion
  14.9 1.2 dynamic-slice
  16.1 23.7 %all-reduce = f32[8,8,32]{2,0,1:T(8,128)S(1)} all-reduce(f32[8,8,32]{2,0,1:T(8,128)S(1)} %copy.23), channel_id=2, replica_groups=mesh['pair_0'=8,'pair_1'=4,'occ'=8] {'occ'}, use_global_device_ids=true, to_apply=%region_2.3.clone | all-reduce | flops 2048 | bytes 16384
  39.8 0.6 dynamic-slice_bitcast_fusion
  40.4 54.3 %all-gather.6.cloned.1.call-done = bf16[32,512,128]{2,1,0:T(8,128)(2,1)} async-done(((bf16[1,512,128]{2,1,0:T(8,128)(2,1)}), bf16[32,512,128]{2,1,0:T(8,128)(2,1)}) %all-gather.6.cloned.1.call-update) | async-done | bytes 4194320 | tf_op jit(solution)/shard_map/all_gather | solution.py:37
  94.7 10.3 %convolution_bitcast_fusion = f32[8,32,128,128]{2,3,0,1:T(8,128)} fusion(bf16[8,512,128,1]{2,1,0,3:T(8,128)(2,1)S(1)} %bitcast.44, bf16[32,512,128]{2,1,0:T(8,128)(2,1)} %all-gather.6.cloned.1.call-done), kind=kOutput, calls=%fused_computation.10 | convolution fusion | flops 4294967296 | bytes 22020096 | tf_op jit(solution)/shard_map/pfa,qfb->pqab/dot_general | solution.py:42
  105.0 66.8 %all-gather.4.cloned.1.call-done = f32[32,128,128]{2,1,0:T(8,128)} async-done(((f32[1,128,128]{2,1,0:T(8,128)}), f32[32,128,128]{2,1,0:T(8,128)}) %all-gather.4.cloned.1.call-update) | async-done | bytes 2097168 | tf_op jit(solution)/shard_map/all_gather | solution.py:49
  171.8 15.3 %fusion.6 = f32[32,128,8,128]{3,1,0,2:T(8,128)} fusion(f32[8,32,128,128]{2,3,0,1:T(8,128)} %convolution_bitcast_fusion, f32[32,128,128]{2,1,0:T(8,128)} %all-gather.4.cloned.1.call-done), kind=kOutput, calls=%fused_computation.8 | convolution fusion | flops 3221225472 | bytes 35651584 | tf_op jit(solution)/shard_map/pqab,qbd->pqad/dot_general | solution.py:50
  187.1 0.0 copy-start.2
  187.1 21.0 %fusion.13 = f32[8,128,128]{2,1,0:T(8,128)} fusion(f32[8,32,128,128]{2,3,0,1:T(8,128)} %convolution_bitcast_fusion, f32[32,128,8,128]{3,1,0,2:T(8,128)} %fusion.6, f32[8,32]{1,0:T(8,128)S(1)} %dynamic-slice_bitcast_fusion), kind=kOutput, calls=%fused_computation.17 | convolution fusion | flops 3225419776 | bytes 34079744 | tf_op jit(solution)/shard_map/pqad,pqed->pae/dot_general | solution.py:52
  208.1 0.0 reduce-scatter.3.cloned.1.call-update
  208.1 0.0 all-gather.8.cloned.1.call-start
  208.2 0.0 copy-done.2
  208.2 0.7 dynamic_slice.25
  208.9 0.0 copy-done
  208.9 31.6 %reduce-scatter.3.cloned.1.call-done = f32[1,128,128]{2,1,0:T(8,128)} async-done(((f32[8,128,128]{2,1,0:T(8,128)}), f32[1,128,128]{2,1,0:T(8,128)}) %reduce-scatter.3.cloned.1.call-update) | async-done | bytes 65552 | tf_op jit(solution)/shard_map/reduce_scatter | solution.py:53
  240.5 2.3 divide_subtract_fusion.1
  242.8 0.0 all-gather.8.cloned.1.call-update
  242.8 0.0 reduce-scatter.5.cloned.1.call-start
  242.9 76.2 %all-gather.8.cloned.1.call-done = f32[32,128,128]{2,1,0:T(8,128)} async-done(((f32[1,128,128]{2,1,0:T(8,128)}), f32[32,128,128]{2,1,0:T(8,128)}) %all-gather.8.cloned.1.call-update) | async-done | bytes 2097168 | tf_op jit(solution)/shard_map/all_gather | solution.py:49
  319.1 15.3 %fusion.3 = f32[32,128,8,128]{3,1,0,2:T(8,128)} fusion(f32[8,32,128,128]{2,3,0,1:T(8,128)} %convolution_bitcast_fusion, f32[32,128,128]{2,1,0:T(8,128)} %all-gather.8.cloned.1.call-done), kind=kOutput, calls=%fused_computation.5 | convolution fusion | flops 3221225472 | bytes 35651584 | tf_op jit(solution)/shard_map/pqab,qbd->pqad/dot_general | solution.py:50
  334.4 0.0 copy-start.1
  334.4 21.0 %fusion.16 = f32[8,128,128]{2,1,0:T(8,128)} fusion(f32[8,32,128,128]{2,3,0,1:T(8,128)} %convolution_bitcast_fusion, f32[32,128,8,128]{3,1,0,2:T(8,128)} %fusion.3, f32[8,32]{1,0:T(8,128)S(1)} %dynamic-slice_bitcast_fusion), kind=kOutput, calls=%fused_computation.18 | convolution fusion | flops 3225419776 | bytes 34079744 | tf_op jit(solution)/shard_map/pqad,pqed->pae/dot_general | solution.py:52
  355.4 0.0 reduce-scatter.5.cloned.1.call-update
  355.4 32.4 %reduce-scatter.5.cloned.1.call-done = f32[1,128,128]{2,1,0:T(8,128)} async-done(((f32[8,128,128]{2,1,0:T(8,128)}), f32[1,128,128]{2,1,0:T(8,128)}) %reduce-scatter.5.cloned.1.call-update) | async-done | bytes 65552 | tf_op jit(solution)/shard_map/reduce_scatter | solution.py:53
  387.8 0.0 copy-done.1
  387.8 1.7 divide_subtract_fusion
  389.5 15.9 %all_gather.23 = f32[8,128,128]{2,1,0:T(8,128)S(1)} all-gather(f32[1,128,128]{2,1,0:T(8,128)S(1)} %get-tuple-element.2), channel_id=1, replica_groups=mesh['pair_0'=8,'pair_1'=4,'occ'=8] {'occ'}, dimensions={0}, use_global_device_ids=true | all-gather | bytes 589824 | tf_op jit(solution)/shard_map/all_gather | solution.py:56
  405.4 13.1 %all_gather.24 = f32[8,128,128]{2,1,0:T(8,128)S(1)} all-gather(f32[1,128,128]{2,1,0:T(8,128)S(1)} %get-tuple-element.3), channel_id=1, replica_groups=mesh['pair_0'=8,'pair_1'=4,'occ'=8] {'occ'}, dimensions={0}, use_global_device_ids=true | all-gather | bytes 589824 | tf_op jit(solution)/shard_map/all_gather | solution.py:56
  418.5 0.8 copy.63
  419.3 0.8 copy.64
  (3 shorter events, 0.0 us)
Async XLA Ops:
  7.2 201.7 %copy-start = (f32[8,128]{1,0:T(8,128)S(1)}, f32[8,128]{1,0:T(8,128)}, u32[]{:S(2)}) copy-start(f32[8,128]{1,0:T(8,128)} %param.11) | copy-start | bytes 12292
  7.2 87.5 %all-gather.6.cloned.1.call-start = ((), (), s32[]{:S(2)}) async-start(), calls=%async_computation.3 | async-start | bytes 4325376 | tf_op jit(solution)/shard_map/all_gather | solution.py:37
  11.5 160.3 %all-gather.4.cloned.1.call-start = ((), (), s32[]{:S(2)}) async-start(), calls=%async_computation.2 | async-start | bytes 2162688 | tf_op jit(solution)/shard_map/all_gather | solution.py:49
  13.1 227.4 %reduce-scatter.3.cloned.1.call-start = ((), (), s32[]{:S(2)}) async-start(), calls=%async_computation.4 | async-start | bytes 589824 | tf_op jit(solution)/shard_map/reduce_scatter | solution.py:53
  187.1 21.1 %copy-start.2 = (f32[8]{0:T(128)S(1)}, f32[8]{0:T(128)}, u32[]{:S(2)}) copy-start(f32[8]{0:T(128)} %param.12) | copy-start | bytes 100
  208.1 110.9 %all-gather.8.cloned.1.call-start = ((), (), s32[]{:S(2)}) async-start(), calls=%async_computation.5 | async-start | bytes 2162688 | tf_op jit(solution)/shard_map/all_gather | solution.py:49
  242.8 145.0 %reduce-scatter.5.cloned.1.call-start = ((), (), s32[]{:S(2)}) async-start(), calls=%async_computation.6 | async-start | bytes 589824 | tf_op jit(solution)/shard_map/reduce_scatter | solution.py:53
  334.4 53.4 %copy-start.1 = (f32[1,128,128]{2,1,0:T(8,128)S(1)}, f32[1,128,128]{2,1,0:T(8,128)}, u32[]{:S(2)}) copy-start(f32[1,128,128]{2,1,0:T(8,128)} %divide_subtract_fusion.1) | copy-start | bytes 196612
Sparse Core Ops, SparseCore 0:
  11.7 82.9 all-gather.5
  97.9 73.9 all-gather.3
  208.3 32.1 reduce-scatter.2
  243.8 75.2 all-gather.7
  355.6 32.1 reduce-scatter.4

commit v2 on v1

v2 whole, which is shorter than its diff:
```python
import jax
import jax.numpy as jnp
from jax import lax
from jax.experimental import pallas as pl
from jax.experimental.pallas import tpu as pltpu
from jax.sharding import Mesh
from jax.sharding import PartitionSpec as P

F32, BF16 = jnp.float32, jnp.bfloat16
NZ, NY, NX, NC = 8, 4, 4, 2
OWNERS, PEERS = NZ * NY, NX * NC
N = 128
TILES = 4
DOMAIN = TILES * N
PAIRS = 8
ROWS = PAIRS * N
CHUNK = 512
AXES = ("z", "y", "x", "core")
PAIR, OCC = ("z", "y"), ("x", "core")


def split(x):
    high = x.astype(BF16)
    return high, (x - high.astype(F32)).astype(BF16)


def push(src, dst, send, recv, device):
    return pltpu.make_async_remote_copy(
        src_ref=src, dst_ref=dst, send_sem=send, recv_sem=recv,
        device_id=device, device_id_type=pl.DeviceIdType.MESH,
    )


class Place:
    def __init__(self):
        self.z, self.y = lax.axis_index("z"), lax.axis_index("y")
        self.occ = lax.axis_index("x") * NC + lax.axis_index("core")
        self.me = self.z * NY + self.y

    def z_to(self, d):
        return {"z": lax.rem(self.z + d + NZ, NZ)}

    def y_to(self, d):
        return {"y": lax.rem(self.y + d + NY, NY)}

    def peer(self, j):
        other = lax.rem(self.occ + j + PEERS, PEERS)
        return other, {"x": other // NC, "core": lax.rem(other, NC)}

    def sign(self, k):
        return 2 * lax.rem(k, 2) - 1

    def row(self, k):
        return lax.rem(self.z + self.sign(k) * ((k + 1) // 2) + NZ, NZ)

    def slot(self, k, dy):
        return self.row(k) * NY + lax.rem(self.y + dy + NY, NY)


class Gather:
    def __init__(self, at, buf, base, rows, zs, zr, ys, yr):
        self.at, self.buf, self.base, self.rows = at, buf, base, rows
        self.zs, self.zr, self.ys, self.yr = zs, zr, ys, yr

    def piece(self, slot, half):
        n = self.rows if half is None else self.rows // 2
        return self.buf.at[slot, pl.ds(self.base + (n if half == 1 else 0), n)]

    def copy(self, axis, slot, half, index, d):
        part = self.piece(slot, half)
        if axis == "z":
            return push(part, part, self.zs.at[index], self.zr.at[index], self.at.z_to(d))
        return push(part, part, self.ys.at[index], self.yr.at[index], self.at.y_to(d))

    def along_z(self, k, slot, tail):
        at, d = self.at, -self.at.sign(k)

        @pl.when(k < 7)
        def _():
            self.copy("z", slot, None, (k,) + tail, d).wait_recv()

        @pl.when(k < 5)
        def _():
            self.copy("z", slot, None, (k + 2,) + tail, d).start()

        @pl.when(k == 5)
        def _():
            self.copy("z", slot, 0, (7,) + tail, -1).start()

        @pl.when(k == 6)
        def _():
            self.copy("z", slot, 1, (8,) + tail, 1).start()

        @pl.when(k == 7)
        def _():
            self.copy("z", slot, 0, (7,) + tail, -1).wait_recv()
            self.copy("z", slot, 1, (8,) + tail, 1).wait_recv()

    def both_z(self, slot, tail):
        self.copy("z", slot, None, (1,) + tail, -1).start()
        self.copy("z", slot, None, (2,) + tail, 1).start()

    def sent_z(self, tail):
        for k in range(1, 7):
            self.copy("z", 0, None, (k,) + tail, 1).wait_send()
        self.copy("z", 0, 0, (7,) + tail, 1).wait_send()
        self.copy("z", 0, 1, (8,) + tail, 1).wait_send()


class ZFirst(Gather):
    def start(self):
        self.both_z(self.at.me, ())
        self.both_y(0)

    def both_y(self, k):
        slot = self.at.slot(k, 0)
        self.copy("y", slot, None, (k, 0), -1).start()
        self.copy("y", slot, None, (k, 1), 1).start()

    def take_z(self, k):
        self.along_z(k, self.at.slot(k, 0), ())
        self.both_y(k)

    def take_y(self, k):
        slot = self.at.slot(k, 1)
        self.copy("y", slot, None, (k, 0), -1).wait_recv()
        self.copy("y", slot, 0, (k, 2), -1).start()
        slot = self.at.slot(k, -1)
        self.copy("y", slot, None, (k, 1), 1).wait_recv()
        self.copy("y", slot, 1, (k, 3), 1).start()

    def last_y(self, k):
        slot = self.at.slot(k, 2)
        self.copy("y", slot, 0, (k, 2), -1).wait_recv()
        self.copy("y", slot, 1, (k, 3), 1).wait_recv()

    def sent(self):
        self.sent_z(())

        @pl.loop(0, NZ)
        def _(k):
            for index, half in enumerate((None, None, 0, 1)):
                self.copy("y", 0, half, (k, index), 1).wait_send()


class YFirst(Gather):
    def start(self):
        me = self.at.me
        self.copy("y", me, None, (0,), -1).start()
        self.copy("y", me, None, (1,), 1).start()
        self.both_z(me, (0,))

    def take_y(self):
        slot = self.at.slot(0, 1)
        self.copy("y", slot, None, (0,), -1).wait_recv()
        self.copy("y", slot, 0, (2,), -1).start()
        self.both_z(slot, (1,))
        slot = self.at.slot(0, -1)
        self.copy("y", slot, None, (1,), 1).wait_recv()
        self.copy("y", slot, 1, (3,), 1).start()
        self.both_z(slot, (2,))
        slot = self.at.slot(0, 2)
        self.copy("y", slot, 0, (2,), -1).wait_recv()
        self.copy("y", slot, 1, (3,), 1).wait_recv()
        self.both_z(slot, (3,))

    def take_z(self, k):
        for j, dy in enumerate((0, 1, -1, 2)):
            self.along_z(k, self.at.slot(k, dy), (j,))

    def sent(self):
        for index, half in enumerate((None, None, 0, 1)):
            self.copy("y", 0, half, (index,), 1).wait_send()
        for j in range(NY):
            self.sent_z((j,))


class Spread:
    def __init__(self, at, out, into, send, recv):
        self.at, self.out, self.into, self.send, self.recv = at, out, into, send, recv

    def copy(self, j):
        other, device = self.at.peer(j)
        return push(self.out(other), self.into.at[self.at.occ], self.send.at[j], self.recv.at[j], device)

    def start(self):
        for j in range(1, PEERS):
            self.copy(j).start()

    def arrived(self):
        for j in range(1, PEERS):
            self.copy(j).wait_recv()

    def sent(self):
        for j in range(1, PEERS):
            self.copy(j).wait_send()


def kernel(
    amp_hbm, exch_hbm, energy_ref, shift_ref, coef_ref, tiles_ref, pair_ref, weight_ref,
    final_ref, residual_ref,
    flipped, coef_all, amp_all, amp_next, high, low, inner, total,
    sums, sums_next, current_all, residual_all, table_out, table_in, table,
    amp_own, exch_own,
    own_sem, c_zs, c_zr, c_ys, c_yr, t_zs, t_zr, t_ys, t_yr,
    n_zs, n_zr, n_ys, n_yr, m_zs, m_zr, m_ys, m_yr, peer_send, peer_recv,
):
    at = Place()
    fetch = [
        pltpu.make_async_copy(amp_hbm.at[at.occ], amp_own, own_sem.at[0]),
        pltpu.make_async_copy(exch_hbm.at[at.occ], exch_own, own_sem.at[1]),
    ]
    for copy in fetch:
        copy.start()

    barrier = pltpu.get_barrier_semaphore()
    for device in (at.z_to(-1), at.z_to(1), at.y_to(-1), at.y_to(1)):
        pl.semaphore_signal(barrier, inc=1, device_id=device, device_id_type=pl.DeviceIdType.MESH)
    for j in range(1, PEERS):
        pl.semaphore_signal(barrier, inc=1, device_id=at.peer(j)[1], device_id_type=pl.DeviceIdType.MESH)

    def ordered(p, t):
        tile = jnp.zeros((N, N), F32)
        for b in range(TILES):
            same = jnp.where(tiles_ref[p, b] == t, 1.0, 0.0)
            tile += coef_ref[p, b * N : (b + 1) * N, :].astype(F32) * same
        return tile.astype(BF16)

    for t in range(TILES):
        coef_all[at.me, t * N : (t + 1) * N, :] = ordered(at.occ, t)
    lane = lax.broadcasted_iota(jnp.int32, (PAIRS, N), 1) * PAIRS
    for place in range(PAIRS):
        piece = jnp.zeros((PAIRS, N), F32)
        for c in range(pair_ref.shape[1]):
            named = jnp.broadcast_to(pair_ref[:, c : c + 1], (PAIRS, N)) == lane + place
            piece += jnp.where(named, jnp.broadcast_to(weight_ref[:, c : c + 1], (PAIRS, N)), 0.0)
        table_out[place] = piece
    table_in[at.occ] = table_out[at.occ]
    for copy in fetch:
        copy.wait()
    amp_all[at.me] = amp_own[...]
    pl.semaphore_wait(barrier, 4 + PEERS - 1)

    coefs = ZFirst(at, coef_all, 0, DOMAIN, c_zs, c_zr, c_ys, c_yr)
    amps = YFirst(at, amp_all, 0, N, t_zs, t_zr, t_ys, t_yr)
    tables = Spread(at, lambda other: table_out.at[other], table_in, peer_send.at[0], peer_recv.at[0])
    coefs.start()
    amps.start()
    tables.start()

    @pl.loop(0, PAIRS)
    def _(p):
        for t in range(TILES):
            flipped[pl.ds(p * N, N), t * N : (t + 1) * N] = ordered(p, t).T

    tables.arrived()
    weights = table_in[0]
    for other in range(1, PEERS):
        weights += table_in[other]
    for owner in range(OWNERS):
        table[owner] = jnp.broadcast_to(weights[:, owner : owner + 1], (PAIRS, N))
    amps.take_y()

    def overlaps(base):
        for pair in range(0, NY, 2):
            theirs = jnp.concatenate([coef_all[base + pair], coef_all[base + pair + 1]], axis=1)
            for first in range(0, ROWS, CHUNK):
                rows = slice(first, first + CHUNK)
                s = jnp.dot(flipped[rows, :], theirs, preferred_element_type=F32)
                up, down = split(s)
                for i in range(2):
                    high[base + pair + i, rows, :] = up[:, i * N : (i + 1) * N]
                    low[base + pair + i, rows, :] = down[:, i * N : (i + 1) * N]

    def couple(base, amplitudes):
        for y in range(NY):
            slot = base + y
            both = jnp.concatenate(split(amplitudes[slot]), axis=1)
            both = jnp.concatenate([both, both], axis=0)
            for first in range(0, ROWS, CHUNK):
                rows = slice(first, first + CHUNK)
                s = jnp.concatenate([high[slot, rows, :], low[slot, rows, :]], axis=1)
                u = jnp.dot(s, both, preferred_element_type=F32)
                u = (u[:, :N] + u[:, N:]).reshape(CHUNK // N, N, N)
                u = u * table[slot, first // N : (first + CHUNK) // N, :][:, None, :]
                up, down = split(u.reshape(CHUNK, N))
                inner[y, rows, :N] = up
                inner[y, rows, N:] = down

        @pl.loop(0, PAIRS)
        def _(p):
            rows = pl.ds(pl.multiple_of(p * N, N), N)
            left = jnp.concatenate([inner[y, rows, :] for y in range(NY)], axis=1)
            right = []
            for y in range(NY):
                up, down = high[base + y, rows, :], low[base + y, rows, :]
                right.append(jnp.concatenate([up, down], axis=0))
                right.append(right[-1])
            out = lax.dot_general(
                left, jnp.concatenate(right, axis=1), (((1,), (1,)), ((), ())),
                preferred_element_type=F32,
            )
            total[p] += out[:, :N] + out[:, N:]

    def denominator(p):
        line = jnp.broadcast_to(energy_ref[pl.ds(p, 1), :], (N, N))
        return line.T + line + shift_ref[p]

    def gathered(into, index):
        spread = Spread(at, lambda other: total.at[other], into, peer_send.at[index], peer_recv.at[index])
        spread.start()
        spread.arrived()
        coupled = total[at.occ]
        for j in range(1, PEERS):
            coupled += into[at.peer(-j)[0]]
        spread.sent()
        return coupled

    total[...] = jnp.zeros_like(total)

    @pl.loop(0, NZ)
    def _(k):
        @pl.when(k < NZ - 1)
        def _():
            coefs.take_z(k + 1)

        coefs.take_y(k)

        @pl.when(k < NZ - 1)
        def _():
            amps.take_z(k + 1)

        coefs.last_y(k)
        base = at.row(k) * NY
        overlaps(base)
        couple(base, amp_all)

    coupled = gathered(sums, 1)
    below = denominator(at.occ)
    current = amp_own[...]
    current = current - (exch_own[...] + below * current - coupled) / below
    amp_next[at.me] = current
    current_all[at.occ] = current
    total[...] = jnp.zeros_like(total)

    late = ZFirst(at, amp_next, N // 2, N // 2, m_zs, m_zr, m_ys, m_yr)
    early = YFirst(at, amp_next, 0, N // 2, n_zs, n_zr, n_ys, n_yr)
    currents = Spread(at, lambda other: current_all.at[at.occ], current_all, peer_send.at[2], peer_recv.at[2])
    late.start()
    early.start()
    early.take_y()
    currents.start()

    @pl.loop(0, NZ)
    def _(k):
        @pl.when(k < NZ - 1)
        def _():
            late.take_z(k + 1)

        late.take_y(k)

        @pl.when(k < NZ - 1)
        def _():
            early.take_z(k + 1)

        late.last_y(k)
        couple(at.row(k) * NY, amp_next)

    coupled = gathered(sums_next, 3)
    current = current_all[at.occ]
    residual_all[at.occ] = exch_own[...] + below * current - coupled
    residuals = Spread(at, lambda other: residual_all.at[at.occ], residual_all, peer_send.at[4], peer_recv.at[4])
    residuals.start()
    currents.arrived()
    residuals.arrived()

    @pl.loop(0, PAIRS)
    def _(p):
        residual = residual_all[p]
        residual_ref[p] = residual
        final_ref[p] = current_all[p] - residual / denominator(p)

    for copies in (coefs, amps, tables, late, early, currents, residuals):
        copies.sent()


def gather_sems():
    dma = pltpu.SemaphoreType.DMA
    z_first = [dma((9,)), dma((9,)), dma((NZ, 4)), dma((NZ, 4))]
    y_first = [dma((9, NY)), dma((9, NY)), dma((4,)), dma((4,))]
    return z_first + y_first + y_first + z_first


def local(
    amplitudes,
    exchange_ints,
    pno_energy,
    pair_shift,
    coefficients,
    domain_tiles,
    couple_owner,
    couple_index,
    couple_weight,
):
    coupled_pair = couple_owner[0, :, :, 0] * PAIRS + couple_index[0]
    vmem, smem, hbm = (
        pl.BlockSpec(memory_space=s) for s in (pltpu.VMEM, pltpu.SMEM, pl.ANY)
    )
    block = (N, N)
    out = jax.ShapeDtypeStruct((PAIRS, N, N), F32)
    return pl.pallas_call(
        kernel,
        out_shape=(out, out),
        in_specs=[hbm, hbm, vmem, smem, vmem, smem, vmem, vmem],
        out_specs=(vmem, vmem),
        scratch_shapes=[
            pltpu.VMEM((ROWS, DOMAIN), BF16),
            pltpu.VMEM((OWNERS, DOMAIN, N), BF16),
            pltpu.VMEM((OWNERS,) + block, F32),
            pltpu.VMEM((OWNERS,) + block, F32),
            pltpu.VMEM((OWNERS, ROWS, N), BF16),
            pltpu.VMEM((OWNERS, ROWS, N), BF16),
            pltpu.VMEM((NY, ROWS, 2 * N), BF16),
            pltpu.VMEM((PAIRS,) + block, F32),
            pltpu.VMEM((PEERS,) + block, F32),
            pltpu.VMEM((PEERS,) + block, F32),
            pltpu.VMEM((PAIRS,) + block, F32),
            pltpu.VMEM((PAIRS,) + block, F32),
            pltpu.VMEM((PEERS, PAIRS, N), F32),
            pltpu.VMEM((PEERS, PAIRS, N), F32),
            pltpu.VMEM((OWNERS, PAIRS, N), F32),
            pltpu.VMEM(block, F32),
            pltpu.VMEM(block, F32),
            pltpu.SemaphoreType.DMA((2,)),
            *gather_sems(),
            pltpu.SemaphoreType.DMA((5, PEERS)),
            pltpu.SemaphoreType.DMA((5, PEERS)),
        ],
        compiler_params=pltpu.CompilerParams(
            collective_id=0, has_side_effects=True, vmem_limit_bytes=52 << 20
        ),
    )(
        amplitudes, exchange_ints, pno_energy, pair_shift, coefficients, domain_tiles,
        coupled_pair, couple_weight[0],
    )


def solution(mesh):
    grid = Mesh(mesh.devices.reshape(NZ, NY, NX, NC), AXES)
    in_specs = (
        P(PAIR, None, None),
        P(PAIR, None, None),
        P(PAIR, None),
        P(PAIR),
        P(PAIR, None, None),
        P(PAIR, None),
        P(OCC, PAIR, None, None),
        P(OCC, PAIR, None),
        P(OCC, PAIR, None),
    )
    out_specs = (P(PAIR, None, None), P(PAIR, None, None))
    return jax.shard_map(local, mesh=grid, in_specs=in_specs, out_specs=out_specs, check_vma=False)
```

time: 427 us -> 185 us (0.43)
  waiting for transfers between devices: 261 us -> 0 us
  Pallas kernels: 0 us -> 180 us
  matrix products: 82.9 us -> 0 us
  blocking collectives: 52.7 us -> 0 us
  between operations: 13.9 us -> 0.68 us
  other arithmetic: 8.49 us -> 0.01 us
    all_gather x3 -> x0, waiting for transfers between devices: 197 us -> none  [the longest x2 143 us: local(): amps = lax.all_gather(current, PAIR)]
    pallas_call x0 -> x1, Pallas kernels: none -> 180 us  [local(): pl.pallas_call(kernel, out_shape=(out, out), in_specs=[hbm, hbm, vmem, sm...]
    dot_general x5 -> x0, matrix products: 82.9 us -> none  [the longest x2 42 us: local(): jnp.einsum('pqad,pqed->pae', inner, overlap, precision=lax.Precision.HIGH)]
    reduce_scatter x2 -> x0, waiting for transfers between devices: 64 us -> none  [local(): coupled = lax.psum_scatter(part, 'occ', scatter_dimension=0, tiled=True)[0]]
    all_gather x2 -> x0, blocking collectives: 29 us -> none  [local(): return (lax.all_gather(current, 'occ'), lax.all_gather(residual, 'occ'))]
    unnamed x1 -> x0, blocking collectives: 23.7 us -> none
  transfers between devices with their start and end apart: 5 -> 0, of which waited for: 5 -> 0; matrix products, arithmetic and copies ran while one was open for 4% -> 0% of each run, Pallas kernels for 0% -> 0%
where the time goes in v2:
time: 185 us
  Pallas kernels  180 us (97%)
  local copies, waits for them, and re-layouts  4.09 us (2%)
    pallas_call x1, Pallas kernels, local(): pl.pallas_call(kernel, out_shape=(out, out), in_specs=[hbm, hbm, vmem, sm...  180 us
    unnamed x15, local copies, waits for them, and re-layouts  4.09 us

profile of v2, /device:TPU:1, one launch (start us, length us, event | category | flops | bytes accessed | tf_op | source)
XLA Modules:
  0.0 184.9 jit_solution(17284759733171284253)
XLA Ops:
  0.6 0.0 copy-start.5
  0.6 0.0 copy-start.4
  0.7 0.8 copy.12.tiles_ref
  1.4 0.0 copy-done.5
  1.4 0.0 copy-done.4
  1.4 0.0 copy-start.1
  1.4 0.0 copy-start.2
  1.4 0.0 copy-start.3
  1.5 0.7 copy-done.1
  2.1 0.0 copy-done.2
  2.1 0.0 copy-done.3
  2.1 0.0 copy-start
  2.1 1.0 copy-done
  3.2 180.1 %shard_map.104 = (f32[8,128,128]{2,1,0:T(8,128)S(1)}, f32[8,128,128]{2,1,0:T(8,128)S(1)}) custom-call(f32[8,128,128]{2,1,0:T(8,128)S(1)} %copy-done, f32[8,128,128]{2,1,0:T(8,128)} %exch_hbm.1, f32[8,128]{1,0:T(8,128)S(1)} %copy-done.1, f32[8]{0:T(128)S(1)} %copy-done.3, bf16[8,512,128]{2,1,0:T(8,128)(2,1)} %coef_ref.1, s32[8,4]{1,0:T(8,128)S(1)} %copy.12.tiles_ref, ...), custom_call_target="tpu_custom_call" | custom-call | tf_op jit(solution)/shard_map/pallas_call | solution.py:411
  183.3 0.8 copy.15
  184.1 0.8 copy.16
  (1 shorter events, 0.0 us)
Async XLA Ops:
  0.6 0.8 copy-start.5
  0.6 0.8 copy-start.4
  1.4 0.7 copy-start.1
  1.4 0.7 copy-start.2
  1.4 0.7 copy-start.3
  2.1 1.0 copy-start

commit v3 on v2

--- a/solution.py
+++ b/solution.py
@@ -199,7 +199,7 @@
 def kernel(
     amp_hbm, exch_hbm, energy_ref, shift_ref, coef_ref, tiles_ref, pair_ref, weight_ref,
     final_ref, residual_ref,
-    flipped, coef_all, amp_all, amp_next, high, low, inner, total,
+    flipped, straight, coef_all, turned, amp_all, amp_next, high, low, high_t, low_t, up_all, down_all, total,
     sums, sums_next, current_all, residual_all, table_out, table_in, table,
     amp_own, exch_own,
     own_sem, c_zs, c_zr, c_ys, c_yr, t_zs, t_zr, t_ys, t_yr,
@@ -251,15 +251,22 @@
     @pl.loop(0, PAIRS)
     def _(p):
         for t in range(TILES):
-            flipped[pl.ds(p * N, N), t * N : (t + 1) * N] = ordered(p, t).T
-
+            tile = ordered(p, t)
+            straight[t * N : (t + 1) * N, pl.ds(pl.multiple_of(p * N, N), N)] = tile
+            flipped[pl.ds(pl.multiple_of(p * N, N), N), t * N : (t + 1) * N] = tile.T
+
+    coefs.take_z(1)
+    coefs.take_z(2)
+    amps.take_y()
+    coefs.take_y(0)
+    amps.take_z(1)
+    amps.take_z(2)
     tables.arrived()
     weights = table_in[0]
     for other in range(1, PEERS):
         weights += table_in[other]
     for owner in range(OWNERS):
         table[owner] = jnp.broadcast_to(weights[:, owner : owner + 1], (PAIRS, N))
-    amps.take_y()
 
     def overlaps(base):
         for pair in range(0, NY, 2):
@@ -271,6 +278,15 @@
                 for i in range(2):
                     high[base + pair + i, rows, :] = up[:, i * N : (i + 1) * N]
                     low[base + pair + i, rows, :] = down[:, i * N : (i + 1) * N]
+        for y in range(NY):
+            for t in range(TILES):
+                part = slice(t * N, (t + 1) * N)
+                turned[y * N : (y + 1) * N, part] = coef_all[base + y, part, :].T
+        theirs = pl.ds(pl.multiple_of(base * N, NY * N), NY * N)
+        for first in range(0, ROWS, 2 * N):
+            cols = slice(first, first + 2 * N)
+            s = jnp.dot(turned[...], straight[:, cols], preferred_element_type=F32)
+            high_t[theirs, cols], low_t[theirs, cols] = split(s)
 
     def couple(base, amplitudes):
         for y in range(NY):
@@ -284,22 +300,17 @@
                 u = (u[:, :N] + u[:, N:]).reshape(CHUNK // N, N, N)
                 u = u * table[slot, first // N : (first + CHUNK) // N, :][:, None, :]
                 up, down = split(u.reshape(CHUNK, N))
-                inner[y, rows, :N] = up
-                inner[y, rows, N:] = down
+                up_all[rows, y * N : (y + 1) * N] = up
+                down_all[rows, y * N : (y + 1) * N] = down
+        theirs = pl.ds(pl.multiple_of(base * N, NY * N), NY * N)
 
         @pl.loop(0, PAIRS)
         def _(p):
-            rows = pl.ds(pl.multiple_of(p * N, N), N)
-            left = jnp.concatenate([inner[y, rows, :] for y in range(NY)], axis=1)
-            right = []
-            for y in range(NY):
-                up, down = high[base + y, rows, :], low[base + y, rows, :]
-                right.append(jnp.concatenate([up, down], axis=0))
-                right.append(right[-1])
-            out = lax.dot_general(
-                left, jnp.concatenate(right, axis=1), (((1,), (1,)), ((), ())),
-                preferred_element_type=F32,
-            )
+            own = pl.ds(pl.multiple_of(p * N, N), N)
+            left = jnp.concatenate([up_all[own, :], down_all[own, :]], axis=0)
+            right = jnp.concatenate([high_t[theirs, own], low_t[theirs, own]], axis=1)
+            out = jnp.dot(left, right, preferred_element_type=F32)
+            out = out[:N] + out[N:]
             total[p] += out[:, :N] + out[:, N:]
 
     def denominator(p):
@@ -320,15 +331,17 @@
 
     @pl.loop(0, NZ)
     def _(k):
-        @pl.when(k < NZ - 1)
-        def _():
-            coefs.take_z(k + 1)
-
-        coefs.take_y(k)
-
-        @pl.when(k < NZ - 1)
-        def _():
-            amps.take_z(k + 1)
+        @pl.when(k + 3 < NZ)
+        def _():
+            coefs.take_z(k + 3)
+
+        @pl.when(k + 1 < NZ)
+        def _():
+            coefs.take_y(k + 1)
+
+        @pl.when(k + 3 < NZ)
+        def _():
+            amps.take_z(k + 3)
 
         coefs.last_y(k)
         base = at.row(k) * NY
@@ -348,20 +361,27 @@
     currents = Spread(at, lambda other: current_all.at[at.occ], current_all, peer_send.at[2], peer_recv.at[2])
     late.start()
     early.start()
+    currents.start()
+    late.take_z(1)
+    late.take_z(2)
     early.take_y()
-    currents.start()
+    late.take_y(0)
+    early.take_z(1)
+    early.take_z(2)
 
     @pl.loop(0, NZ)
     def _(k):
-        @pl.when(k < NZ - 1)
-        def _():
-            late.take_z(k + 1)
-
-        late.take_y(k)
-
-        @pl.when(k < NZ - 1)
-        def _():
-            early.take_z(k + 1)
+        @pl.when(k + 3 < NZ)
+        def _():
+            late.take_z(k + 3)
+
+        @pl.when(k + 1 < NZ)
+        def _():
+            late.take_y(k + 1)
+
+        @pl.when(k + 3 < NZ)
+        def _():
+            early.take_z(k + 3)
 
         late.last_y(k)
         couple(at.row(k) * NY, amp_next)
@@ -371,6 +391,11 @@
     residual_all[at.occ] = exch_own[...] + below * current - coupled
     residuals = Spread(at, lambda other: residual_all.at[at.occ], residual_all, peer_send.at[4], peer_recv.at[4])
     residuals.start()
+
+    @pl.loop(0, PAIRS)
+    def _(p):
+        final_ref[p] = denominator(p)
+
     currents.arrived()
     residuals.arrived()
 
@@ -378,7 +403,7 @@
     def _(p):
         residual = residual_all[p]
         residual_ref[p] = residual
-        final_ref[p] = current_all[p] - residual / denominator(p)
+        final_ref[p] = current_all[p] - residual / final_ref[p]
 
     for copies in (coefs, amps, tables, late, early, currents, residuals):
         copies.sent()
@@ -415,12 +440,17 @@
         out_specs=(vmem, vmem),
         scratch_shapes=[
             pltpu.VMEM((ROWS, DOMAIN), BF16),
+            pltpu.VMEM((DOMAIN, ROWS), BF16),
             pltpu.VMEM((OWNERS, DOMAIN, N), BF16),
+            pltpu.VMEM((NY * N, DOMAIN), BF16),
             pltpu.VMEM((OWNERS,) + block, F32),
             pltpu.VMEM((OWNERS,) + block, F32),
             pltpu.VMEM((OWNERS, ROWS, N), BF16),
             pltpu.VMEM((OWNERS, ROWS, N), BF16),
-            pltpu.VMEM((NY, ROWS, 2 * N), BF16),
+            pltpu.VMEM((OWNERS * N, ROWS), BF16),
+            pltpu.VMEM((OWNERS * N, ROWS), BF16),
+            pltpu.VMEM((ROWS, NY * N), BF16),
+            pltpu.VMEM((ROWS, NY * N), BF16),
             pltpu.VMEM((PAIRS,) + block, F32),
             pltpu.VMEM((PEERS,) + block, F32),
             pltpu.VMEM((PEERS,) + block, F32),
@@ -437,7 +467,7 @@
             pltpu.SemaphoreType.DMA((5, PEERS)),
         ],
         compiler_params=pltpu.CompilerParams(
-            collective_id=0, has_side_effects=True, vmem_limit_bytes=52 << 20
+            collective_id=0, has_side_effects=True, vmem_limit_bytes=58 << 20
         ),
     )(
         amplitudes, exchange_ints, pno_energy, pair_shift, coefficients, domain_tiles,

time: 185 us -> 142 us (0.77)
  Pallas kernels: 180 us -> 137 us
    pallas_call x1, Pallas kernels: 180 us -> 137 us  [local(): pl.pallas_call(kernel, out_shape=(out, out), in_specs=[hbm, hbm, vmem, sm...]
    unnamed x15 -> x9, local copies, waits for them, and re-layouts: 4.09 us -> 4.09 us
where the time goes in v3:
time: 142 us
  Pallas kernels  137 us (96%)
  local copies, waits for them, and re-layouts  4.09 us (3%)
    pallas_call x1, Pallas kernels, local(): pl.pallas_call(kernel, out_shape=(out, out), in_specs=[hbm, hbm, vmem, sm...  137 us
    unnamed x9, local copies, waits for them, and re-layouts  4.09 us

profile of v3, /device:TPU:1, one launch (start us, length us, event | category | flops | bytes accessed | tf_op | source)
XLA Modules:
  0.0 142.0 jit_solution(12633802640315140636)
XLA Ops:
  0.6 0.0 copy-start.2
  0.6 0.0 copy-start.1
  0.7 1.4 copy.12.tiles_ref
  2.0 0.0 copy-done.2
  2.0 0.0 copy-done.1
  2.0 0.6 bitcast_add_fusion.pair_ref
  2.6 136.6 %shard_map.104 = (f32[8,128,128]{2,1,0:T(8,128)}, f32[8,128,128]{2,1,0:T(8,128)}) custom-call(f32[8,128,128]{2,1,0:T(8,128)} %amp_hbm.1, f32[8,128,128]{2,1,0:T(8,128)} %exch_hbm.1, f32[8,128]{1,0:T(8,128)} %energy_ref.1, f32[8]{0:T(128)} %shift_ref.1, bf16[8,512,128]{2,1,0:T(8,128)(2,1)} %coef_ref.1, s32[8,4]{1,0:T(8,128)} %copy.12.tiles_ref, ...), custom_call_target="tpu_custom_call" | custom-call | tf_op jit(solution)/shard_map/pallas_call | solution.py:436
  139.2 0.0 copy-start
  139.3 1.9 %copy.15 = f32[8,128,128]{2,1,0:T(8,128)} copy(f32[8,128,128]{2,1,0:T(8,128)} %get-tuple-element.4) | data formatting | bytes 1048576
  141.2 0.0 copy-done
  141.2 0.8 copy.16
Async XLA Ops:
  0.6 1.4 copy-start.2
  0.6 1.4 copy-start.1
  139.2 1.9 %copy-start = (f32[8,128,128]{2,1,0:T(8,128)S(1)}, f32[8,128,128]{2,1,0:T(8,128)}, u32[]{:S(2)}) copy-start(f32[8,128,128]{2,1,0:T(8,128)} %get-tuple-element.5) | copy-start | bytes 1572868

commit v4 on v3

--- a/solution.py
+++ b/solution.py
@@ -15,6 +15,8 @@
 PAIRS = 8
 ROWS = PAIRS * N
 CHUNK = 512
+EARLY = 48
+LEAD = 3
 AXES = ("z", "y", "x", "core")
 PAIR, OCC = ("z", "y"), ("x", "core")
 
@@ -34,7 +36,8 @@
 class Place:
     def __init__(self):
         self.z, self.y = lax.axis_index("z"), lax.axis_index("y")
-        self.occ = lax.axis_index("x") * NC + lax.axis_index("core")
+        self.x, self.core = lax.axis_index("x"), lax.axis_index("core")
+        self.occ = self.x * NC + self.core
         self.me = self.z * NY + self.y
 
     def z_to(self, d):
@@ -46,6 +49,13 @@
     def peer(self, j):
         other = lax.rem(self.occ + j + PEERS, PEERS)
         return other, {"x": other // NC, "core": lax.rem(other, NC)}
+
+    def x_to(self, d):
+        other = lax.rem(self.x + d + NX, NX)
+        return other, {"x": other}
+
+    def partner(self):
+        return {"core": 1 - self.core}
 
     def sign(self, k):
         return 2 * lax.rem(k, 2) - 1
@@ -196,11 +206,79 @@
             self.copy(j).wait_send()
 
 
+class Sums:
+    def __init__(self, at, total, near, far, send, recv):
+        self.at, self.total, self.near, self.far, self.send, self.recv = at, total, near, far, send, recv
+
+    def inside(self, j):
+        other = self.at.x_to(j)[0]
+        source = self.total.at[other, 1 - self.at.core]
+        return push(source, self.near.at[other], self.send.at[j], self.recv.at[j], self.at.partner())
+
+    def outside(self, j):
+        other, device = self.at.x_to(j)
+        source = self.total.at[other, self.at.core]
+        index = NX + j
+        return push(source, self.far.at[self.at.x], self.send.at[index], self.recv.at[index], device)
+
+    def run(self):
+        at, order = self.at, (2, 1, 3, 0)
+        for j in order:
+            self.inside(j).start()
+        for j in order:
+            other = at.x_to(j)[0]
+            self.inside(j).wait_recv()
+            self.total[other, at.core] += self.near[other]
+            if j:
+                self.outside(j).start()
+        out = self.total[at.x, at.core]
+        for j in (1, 3, 2):
+            self.outside(j).wait_recv()
+            out += self.far[at.x_to(-j)[0]]
+        for j in order:
+            self.inside(j).wait_send()
+            if j:
+                self.outside(j).wait_send()
+        return out
+
+
+class Shares:
+    def __init__(self, at, buf, send, recv):
+        self.at, self.buf, self.send, self.recv = at, buf, send, recv
+
+    def outside(self, j):
+        block = self.buf.at[self.at.x, self.at.core]
+        return push(block, block, self.send.at[j], self.recv.at[j], self.at.x_to(j)[1])
+
+    def inside(self, j):
+        index = NX + j
+        block = self.buf.at[self.at.x_to(-j)[0], self.at.core]
+        return push(block, block, self.send.at[index], self.recv.at[index], self.at.partner())
+
+    def start(self):
+        for j in (2, 1, 3):
+            self.outside(j).start()
+        self.inside(0).start()
+
+    def arrived(self):
+        for j in (1, 3, 2):
+            self.outside(j).wait_recv()
+            self.inside(j).start()
+        for j in range(NX):
+            self.inside(j).wait_recv()
+
+    def sent(self):
+        for j in range(NX):
+            self.inside(j).wait_send()
+            if j:
+                self.outside(j).wait_send()
+
+
 def kernel(
     amp_hbm, exch_hbm, energy_ref, shift_ref, coef_ref, tiles_ref, pair_ref, weight_ref,
     final_ref, residual_ref,
     flipped, straight, coef_all, turned, amp_all, amp_next, high, low, high_t, low_t, up_all, down_all, total,
-    sums, sums_next, current_all, residual_all, table_out, table_in, table,
+    near, near_next, far, far_next, current_all, residual_all, table_out, table_in, table,
     amp_own, exch_own,
     own_sem, c_zs, c_zr, c_ys, c_yr, t_zs, t_zr, t_ys, t_yr,
     n_zs, n_zr, n_ys, n_yr, m_zs, m_zr, m_ys, m_yr, peer_send, peer_recv,
@@ -255,12 +333,12 @@
             straight[t * N : (t + 1) * N, pl.ds(pl.multiple_of(p * N, N), N)] = tile
             flipped[pl.ds(pl.multiple_of(p * N, N), N), t * N : (t + 1) * N] = tile.T
 
-    coefs.take_z(1)
-    coefs.take_z(2)
+    for k in range(1, LEAD):
+        coefs.take_z(k)
     amps.take_y()
     coefs.take_y(0)
-    amps.take_z(1)
-    amps.take_z(2)
+    for k in range(1, LEAD):
+        amps.take_z(k)
     tables.arrived()
     weights = table_in[0]
     for other in range(1, PEERS):
@@ -304,51 +382,37 @@
                 down_all[rows, y * N : (y + 1) * N] = down
         theirs = pl.ds(pl.multiple_of(base * N, NY * N), NY * N)
 
-        @pl.loop(0, PAIRS)
-        def _(p):
-            own = pl.ds(pl.multiple_of(p * N, N), N)
+        for p in range(PAIRS):
+            own = slice(p * N, (p + 1) * N)
             left = jnp.concatenate([up_all[own, :], down_all[own, :]], axis=0)
             right = jnp.concatenate([high_t[theirs, own], low_t[theirs, own]], axis=1)
             out = jnp.dot(left, right, preferred_element_type=F32)
             out = out[:N] + out[N:]
-            total[p] += out[:, :N] + out[:, N:]
+            total[p // NC, p % NC] += out[:, :N] + out[:, N:]
 
     def denominator(p):
         line = jnp.broadcast_to(energy_ref[pl.ds(p, 1), :], (N, N))
         return line.T + line + shift_ref[p]
 
-    def gathered(into, index):
-        spread = Spread(at, lambda other: total.at[other], into, peer_send.at[index], peer_recv.at[index])
-        spread.start()
-        spread.arrived()
-        coupled = total[at.occ]
-        for j in range(1, PEERS):
-            coupled += into[at.peer(-j)[0]]
-        spread.sent()
-        return coupled
-
     total[...] = jnp.zeros_like(total)
 
     @pl.loop(0, NZ)
     def _(k):
-        @pl.when(k + 3 < NZ)
-        def _():
-            coefs.take_z(k + 3)
-
         @pl.when(k + 1 < NZ)
         def _():
             coefs.take_y(k + 1)
 
-        @pl.when(k + 3 < NZ)
-        def _():
-            amps.take_z(k + 3)
+        @pl.when(k + LEAD < NZ)
+        def _():
+            coefs.take_z(k + LEAD)
+            amps.take_z(k + LEAD)
 
         coefs.last_y(k)
         base = at.row(k) * NY
         overlaps(base)
         couple(base, amp_all)
 
-    coupled = gathered(sums, 1)
+    coupled = Sums(at, total, near, far, peer_send.at[1], peer_recv.at[1]).run()
     below = denominator(at.occ)
     current = amp_own[...]
     current = current - (exch_own[...] + below * current - coupled) / below
@@ -356,40 +420,37 @@
     current_all[at.occ] = current
     total[...] = jnp.zeros_like(total)
 
-    late = ZFirst(at, amp_next, N // 2, N // 2, m_zs, m_zr, m_ys, m_yr)
-    early = YFirst(at, amp_next, 0, N // 2, n_zs, n_zr, n_ys, n_yr)
+    late = ZFirst(at, amp_next, EARLY, N - EARLY, m_zs, m_zr, m_ys, m_yr)
+    early = YFirst(at, amp_next, 0, EARLY, n_zs, n_zr, n_ys, n_yr)
     currents = Spread(at, lambda other: current_all.at[at.occ], current_all, peer_send.at[2], peer_recv.at[2])
     late.start()
     early.start()
     currents.start()
-    late.take_z(1)
-    late.take_z(2)
+    for k in range(1, LEAD):
+        late.take_z(k)
     early.take_y()
     late.take_y(0)
-    early.take_z(1)
-    early.take_z(2)
+    for k in range(1, LEAD):
+        early.take_z(k)
 
     @pl.loop(0, NZ)
     def _(k):
-        @pl.when(k + 3 < NZ)
-        def _():
-            late.take_z(k + 3)
-
         @pl.when(k + 1 < NZ)
         def _():
             late.take_y(k + 1)
 
-        @pl.when(k + 3 < NZ)
-        def _():
-            early.take_z(k + 3)
+        @pl.when(k + LEAD < NZ)
+        def _():
+            late.take_z(k + LEAD)
+            early.take_z(k + LEAD)
 
         late.last_y(k)
         couple(at.row(k) * NY, amp_next)
 
-    coupled = gathered(sums_next, 3)
+    coupled = Sums(at, total, near_next, far_next, peer_send.at[3], peer_recv.at[3]).run()
     current = current_all[at.occ]
-    residual_all[at.occ] = exch_own[...] + below * current - coupled
-    residuals = Spread(at, lambda other: residual_all.at[at.occ], residual_all, peer_send.at[4], peer_recv.at[4])
+    residual_all[at.x, at.core] = exch_own[...] + below * current - coupled
+    residuals = Shares(at, residual_all, peer_send.at[4], peer_recv.at[4])
     residuals.start()
 
     @pl.loop(0, PAIRS)
@@ -401,7 +462,7 @@
 
     @pl.loop(0, PAIRS)
     def _(p):
-        residual = residual_all[p]
+        residual = residual_all[p // NC, lax.rem(p, NC)]
         residual_ref[p] = residual
         final_ref[p] = current_all[p] - residual / final_ref[p]
 
@@ -429,7 +490,7 @@
 ):
     coupled_pair = couple_owner[0, :, :, 0] * PAIRS + couple_index[0]
     vmem, smem, hbm = (
-        pl.BlockSpec(memory_space=s) for s in (pltpu.VMEM, pltpu.SMEM, pl.ANY)
+        pl.BlockSpec(memory_space=s) for s in (pltpu.VMEM, pltpu.SMEM, pltpu.HBM)
     )
     block = (N, N)
     out = jax.ShapeDtypeStruct((PAIRS, N, N), F32)
@@ -451,11 +512,13 @@
             pltpu.VMEM((OWNERS * N, ROWS), BF16),
             pltpu.VMEM((ROWS, NY * N), BF16),
             pltpu.VMEM((ROWS, NY * N), BF16),
+            pltpu.VMEM((NX, NC) + block, F32),
+            pltpu.VMEM((NX,) + block, F32),
+            pltpu.VMEM((NX,) + block, F32),
+            pltpu.VMEM((NX,) + block, F32),
+            pltpu.VMEM((NX,) + block, F32),
             pltpu.VMEM((PAIRS,) + block, F32),
-            pltpu.VMEM((PEERS,) + block, F32),
-            pltpu.VMEM((PEERS,) + block, F32),
-            pltpu.VMEM((PAIRS,) + block, F32),
-            pltpu.VMEM((PAIRS,) + block, F32),
+            pltpu.VMEM((NX, NC) + block, F32),
             pltpu.VMEM((PEERS, PAIRS, N), F32),
             pltpu.VMEM((PEERS, PAIRS, N), F32),
             pltpu.VMEM((OWNERS, PAIRS, N), F32),
@@ -467,7 +530,7 @@
             pltpu.SemaphoreType.DMA((5, PEERS)),
         ],
         compiler_params=pltpu.CompilerParams(
-            collective_id=0, has_side_effects=True, vmem_limit_bytes=58 << 20
+            collective_id=0, has_side_effects=True, vmem_limit_bytes=52 << 20
         ),
     )(
         amplitudes, exchange_ints, pno_energy, pair_shift, coefficients, domain_tiles,

time: 142 us -> 120 us (0.85)
  Pallas kernels: 137 us -> 115 us
    pallas_call x1, Pallas kernels: 137 us -> 115 us  [local(): pl.pallas_call(kernel, out_shape=(out, out), in_specs=[hbm, hbm, vmem, sm...]
    unnamed x9 -> x15, local copies, waits for them, and re-layouts: 4.09 us -> 4.09 us
where the time goes in v4:
time: 120 us
  Pallas kernels  115 us (96%)
  local copies, waits for them, and re-layouts  4.09 us (3%)
    pallas_call x1, Pallas kernels, local(): pl.pallas_call(kernel, out_shape=(out, out), in_specs=[hbm, hbm, vmem, sm...  115 us
    unnamed x15, local copies, waits for them, and re-layouts  4.09 us

profile of v4, /device:TPU:1, one launch (start us, length us, event | category | flops | bytes accessed | tf_op | source)
XLA Modules:
  0.0 120.1 jit_solution(9556911870626269839)
XLA Ops:
  0.6 0.0 copy-start.5
  0.6 0.0 copy-start.4
  0.7 0.8 copy.12.tiles_ref
  1.4 0.0 copy-done.5
  1.4 0.0 copy-done.4
  1.4 0.0 copy-start.1
  1.4 0.0 copy-start.2
  1.4 0.0 copy-start.3
  1.5 0.7 copy-done.1
  2.1 0.0 copy-done.2
  2.1 0.0 copy-done.3
  2.1 0.0 copy-start
  2.1 1.0 copy-done
  3.2 115.4 %shard_map.104 = (f32[8,128,128]{2,1,0:T(8,128)S(1)}, f32[8,128,128]{2,1,0:T(8,128)S(1)}) custom-call(f32[8,128,128]{2,1,0:T(8,128)S(1)} %copy-done, f32[8,128,128]{2,1,0:T(8,128)} %exch_hbm.1, f32[8,128]{1,0:T(8,128)S(1)} %copy-done.1, f32[8]{0:T(128)S(1)} %copy-done.3, bf16[8,512,128]{2,1,0:T(8,128)(2,1)} %coef_ref.1, s32[8,4]{1,0:T(8,128)S(1)} %copy.12.tiles_ref, ...), custom_call_target="tpu_custom_call" | custom-call | tf_op jit(solution)/shard_map/pallas_call | solution.py:497
  118.6 0.8 copy.15
  119.3 0.8 copy.16
  (1 shorter events, 0.0 us)
Async XLA Ops:
  0.6 0.8 copy-start.5
  0.6 0.8 copy-start.4
  1.4 0.7 copy-start.1
  1.4 0.7 copy-start.2
  1.4 0.7 copy-start.3
  2.1 1.0 copy-start

commit v5 on v4

--- a/solution.py
+++ b/solution.py
@@ -16,7 +16,6 @@
 ROWS = PAIRS * N
 CHUNK = 512
 EARLY = 48
-LEAD = 3
 AXES = ("z", "y", "x", "core")
 PAIR, OCC = ("z", "y"), ("x", "core")
 
@@ -169,20 +168,58 @@
         self.copy("y", slot, None, (1,), 1).wait_recv()
         self.copy("y", slot, 1, (3,), 1).start()
         self.both_z(slot, (2,))
+
+    def last_y(self):
         slot = self.at.slot(0, 2)
         self.copy("y", slot, 0, (2,), -1).wait_recv()
         self.copy("y", slot, 1, (3,), 1).wait_recv()
         self.both_z(slot, (3,))
 
-    def take_z(self, k):
-        for j, dy in enumerate((0, 1, -1, 2)):
-            self.along_z(k, self.at.slot(k, dy), (j,))
+    def take_z(self, k, ways):
+        for j in ways:
+            self.along_z(k, self.at.slot(k, (0, 1, -1, 2)[j]), (j,))
 
     def sent(self):
         for index, half in enumerate((None, None, 0, 1)):
             self.copy("y", 0, half, (index,), 1).wait_send()
         for j in range(NY):
             self.sent_z((j,))
+
+
+def each(hop, do):
+    for k in (2 * hop - 1, 2 * hop):
+        pl.when(k < NZ)(lambda k=k: do(k))
+
+
+def levels(z_first, y_first, work):
+    z_first.take_z(1)
+    z_first.take_z(2)
+    y_first.take_y()
+    z_first.take_y(0)
+
+    def level(t):
+        each(t - 1, z_first.take_y)
+        pl.when(t <= NZ // 2)(lambda: each(t, z_first.take_z))
+        each(t - 1, lambda k: y_first.take_z(k, (0, 1, 2)))
+
+    level(2)
+    y_first.last_y()
+    z_first.last_y(0)
+    work(0)
+
+    @pl.loop(3, NZ // 2 + 2)
+    def _(t):
+        level(t)
+        each(t - 2, lambda k: y_first.take_z(k, (3,)))
+        each(t - 2, z_first.last_y)
+
+        @pl.loop(2 * t - 5, 2 * t - 3)
+        def _(k):
+            work(k)
+
+    y_first.take_z(NZ - 1, (3,))
+    z_first.last_y(NZ - 1)
+    work(NZ - 1)
 
 
 class Spread:
@@ -333,12 +370,6 @@
             straight[t * N : (t + 1) * N, pl.ds(pl.multiple_of(p * N, N), N)] = tile
             flipped[pl.ds(pl.multiple_of(p * N, N), N), t * N : (t + 1) * N] = tile.T
 
-    for k in range(1, LEAD):
-        coefs.take_z(k)
-    amps.take_y()
-    coefs.take_y(0)
-    for k in range(1, LEAD):
-        amps.take_z(k)
     tables.arrived()
     weights = table_in[0]
     for other in range(1, PEERS):
@@ -396,21 +427,12 @@
 
     total[...] = jnp.zeros_like(total)
 
-    @pl.loop(0, NZ)
-    def _(k):
-        @pl.when(k + 1 < NZ)
-        def _():
-            coefs.take_y(k + 1)
-
-        @pl.when(k + LEAD < NZ)
-        def _():
-            coefs.take_z(k + LEAD)
-            amps.take_z(k + LEAD)
-
-        coefs.last_y(k)
+    def first(k):
         base = at.row(k) * NY
         overlaps(base)
         couple(base, amp_all)
+
+    levels(coefs, amps, first)
 
     coupled = Sums(at, total, near, far, peer_send.at[1], peer_recv.at[1]).run()
     below = denominator(at.occ)
@@ -426,27 +448,7 @@
     late.start()
     early.start()
     currents.start()
-    for k in range(1, LEAD):
-        late.take_z(k)
-    early.take_y()
-    late.take_y(0)
-    for k in range(1, LEAD):
-        early.take_z(k)
-
-    @pl.loop(0, NZ)
-    def _(k):
-        @pl.when(k + 1 < NZ)
-        def _():
-            late.take_y(k + 1)
-
-        @pl.when(k + LEAD < NZ)
-        def _():
-            late.take_z(k + LEAD)
-            early.take_z(k + LEAD)
-
-        late.last_y(k)
-        couple(at.row(k) * NY, amp_next)
-
+    levels(late, early, lambda k: couple(at.row(k) * NY, amp_next))
     coupled = Sums(at, total, near_next, far_next, peer_send.at[3], peer_recv.at[3]).run()
     current = current_all[at.occ]
     residual_all[at.x, at.core] = exch_own[...] + below * current - coupled

time: 120 us -> 109 us (0.908)
  Pallas kernels: 115 us -> 104 us
    pallas_call x1, Pallas kernels: 115 us -> 104 us  [local(): pl.pallas_call(kernel, out_shape=(out, out), in_specs=[hbm, hbm, vmem, sm...]
where the time goes in v5:
time: 109 us
  Pallas kernels  104 us (95%)
  local copies, waits for them, and re-layouts  4.09 us (4%)
    pallas_call x1, Pallas kernels, local(): pl.pallas_call(kernel, out_shape=(out, out), in_specs=[hbm, hbm, vmem, sm...  104 us
    unnamed x15, local copies, waits for them, and re-layouts  4.09 us

profile of v5, /device:TPU:1, one launch (start us, length us, event | category | flops | bytes accessed | tf_op | source)
XLA Modules:
  0.0 108.7 jit_solution(7791833396224137503)
XLA Ops:
  0.6 0.0 copy-start.5
  0.6 0.0 copy-start.4
  0.7 0.8 copy.12.tiles_ref
  1.4 0.0 copy-done.5
  1.4 0.0 copy-done.4
  1.4 0.0 copy-start.1
  1.4 0.0 copy-start.2
  1.4 0.0 copy-start.3
  1.5 0.7 copy-done.1
  2.1 0.0 copy-done.2
  2.1 0.0 copy-done.3
  2.1 0.0 copy-start
  2.1 1.0 copy-done
  3.2 103.9 %shard_map.104 = (f32[8,128,128]{2,1,0:T(8,128)S(1)}, f32[8,128,128]{2,1,0:T(8,128)S(1)}) custom-call(f32[8,128,128]{2,1,0:T(8,128)S(1)} %copy-done, f32[8,128,128]{2,1,0:T(8,128)} %exch_hbm.1, f32[8,128]{1,0:T(8,128)S(1)} %copy-done.1, f32[8]{0:T(128)S(1)} %copy-done.3, bf16[8,512,128]{2,1,0:T(8,128)(2,1)} %coef_ref.1, s32[8,4]{1,0:T(8,128)S(1)} %copy.12.tiles_ref, ...), custom_call_target="tpu_custom_call" | custom-call | tf_op jit(solution)/shard_map/pallas_call | solution.py:499
  107.1 0.8 copy.15
  107.9 0.8 copy.16
  (1 shorter events, 0.0 us)
Async XLA Ops:
  0.6 0.8 copy-start.5
  0.6 0.8 copy-start.4
  1.4 0.7 copy-start.1
  1.4 0.7 copy-start.2
  1.4 0.7 copy-start.3
  2.1 1.0 copy-start

commit v6 on v5

--- a/solution.py
+++ b/solution.py
@@ -198,8 +198,8 @@
     z_first.take_y(0)
 
     def level(t):
+        pl.when(t <= NZ // 2)(lambda: each(t, z_first.take_z))
         each(t - 1, z_first.take_y)
-        pl.when(t <= NZ // 2)(lambda: each(t, z_first.take_z))
         each(t - 1, lambda k: y_first.take_z(k, (0, 1, 2)))
 
     level(2)
@@ -209,8 +209,8 @@
 
     @pl.loop(3, NZ // 2 + 2)
     def _(t):
+        each(t - 2, lambda k: y_first.take_z(k, (3,)))
         level(t)
-        each(t - 2, lambda k: y_first.take_z(k, (3,)))
         each(t - 2, z_first.last_y)
 
         @pl.loop(2 * t - 5, 2 * t - 3)

time: 109 us -> 107 us (0.982)
  Pallas kernels: 104 us -> 102 us
    pallas_call x1, Pallas kernels: 104 us -> 102 us  [local(): pl.pallas_call(kernel, out_shape=(out, out), in_specs=[hbm, hbm, vmem, sm...]
where the time goes in v6:
time: 107 us
  Pallas kernels  102 us (95%)
  local copies, waits for them, and re-layouts  4.09 us (4%)
    pallas_call x1, Pallas kernels, local(): pl.pallas_call(kernel, out_shape=(out, out), in_specs=[hbm, hbm, vmem, sm...  102 us
    unnamed x15, local copies, waits for them, and re-layouts  4.09 us

profile of v6, /device:TPU:1, one launch (start us, length us, event | category | flops | bytes accessed | tf_op | source)
XLA Modules:
  0.0 106.8 jit_solution(7505552476715893807)
XLA Ops:
  0.6 0.0 copy-start.5
  0.6 0.0 copy-start.4
  0.7 0.8 copy.12.tiles_ref
  1.4 0.0 copy-done.5
  1.4 0.0 copy-done.4
  1.4 0.0 copy-start.1
  1.4 0.0 copy-start.2
  1.4 0.0 copy-start.3
  1.5 0.7 copy-done.1
  2.1 0.0 copy-done.2
  2.1 0.0 copy-done.3
  2.1 0.0 copy-start
  2.1 1.0 copy-done
  3.2 102.1 %shard_map.104 = (f32[8,128,128]{2,1,0:T(8,128)S(1)}, f32[8,128,128]{2,1,0:T(8,128)S(1)}) custom-call(f32[8,128,128]{2,1,0:T(8,128)S(1)} %copy-done, f32[8,128,128]{2,1,0:T(8,128)} %exch_hbm.1, f32[8,128]{1,0:T(8,128)S(1)} %copy-done.1, f32[8]{0:T(128)S(1)} %copy-done.3, bf16[8,512,128]{2,1,0:T(8,128)(2,1)} %coef_ref.1, s32[8,4]{1,0:T(8,128)S(1)} %copy.12.tiles_ref, ...), custom_call_target="tpu_custom_call" | custom-call | tf_op jit(solution)/shard_map/pallas_call | solution.py:499
  105.2 0.8 copy.15
  106.0 0.8 copy.16
  (1 shorter events, 0.0 us)
Async XLA Ops:
  0.6 0.8 copy-start.5
  0.6 0.8 copy-start.4
  1.4 0.7 copy-start.1
  1.4 0.7 copy-start.2
  1.4 0.7 copy-start.3
  2.1 1.0 copy-start

commit v7 on v6

--- a/solution.py
+++ b/solution.py
@@ -343,6 +343,16 @@
 
     for t in range(TILES):
         coef_all[at.me, t * N : (t + 1) * N, :] = ordered(at.occ, t)
+    coefs = ZFirst(at, coef_all, 0, DOMAIN, c_zs, c_zr, c_ys, c_yr)
+    amps = YFirst(at, amp_all, 0, N, t_zs, t_zr, t_ys, t_yr)
+    tables = Spread(at, lambda other: table_out.at[other], table_in, peer_send.at[0], peer_recv.at[0])
+    for copy in fetch:
+        copy.wait()
+    amp_all[at.me] = amp_own[...]
+    pl.semaphore_wait(barrier, 4 + PEERS - 1)
+    coefs.start()
+    amps.start()
+
     lane = lax.broadcasted_iota(jnp.int32, (PAIRS, N), 1) * PAIRS
     for place in range(PAIRS):
         piece = jnp.zeros((PAIRS, N), F32)
@@ -351,16 +361,6 @@
             piece += jnp.where(named, jnp.broadcast_to(weight_ref[:, c : c + 1], (PAIRS, N)), 0.0)
         table_out[place] = piece
     table_in[at.occ] = table_out[at.occ]
-    for copy in fetch:
-        copy.wait()
-    amp_all[at.me] = amp_own[...]
-    pl.semaphore_wait(barrier, 4 + PEERS - 1)
-
-    coefs = ZFirst(at, coef_all, 0, DOMAIN, c_zs, c_zr, c_ys, c_yr)
-    amps = YFirst(at, amp_all, 0, N, t_zs, t_zr, t_ys, t_yr)
-    tables = Spread(at, lambda other: table_out.at[other], table_in, peer_send.at[0], peer_recv.at[0])
-    coefs.start()
-    amps.start()
     tables.start()
 
     @pl.loop(0, PAIRS)

time: 107 us -> 107 us (level)
  no operation moved by 1% of the time
where the time goes in v7:
time: 107 us
  Pallas kernels  102 us (95%)
  local copies, waits for them, and re-layouts  4.09 us (4%)
    pallas_call x1, Pallas kernels, local(): pl.pallas_call(kernel, out_shape=(out, out), in_specs=[hbm, hbm, vmem, sm...  102 us
    unnamed x15, local copies, waits for them, and re-layouts  4.09 us

profile of v7, /device:TPU:1, one launch (start us, length us, event | category | flops | bytes accessed | tf_op | source)
XLA Modules:
  0.0 107.1 jit_solution(591418811607016870)
XLA Ops:
  0.6 0.0 copy-start.5
  0.6 0.0 copy-start.4
  0.7 0.8 copy.12.tiles_ref
  1.4 0.0 copy-done.5
  1.4 0.0 copy-done.4
  1.4 0.0 copy-start.1
  1.4 0.0 copy-start.2
  1.4 0.0 copy-start.3
  1.5 0.7 copy-done.1
  2.1 0.0 copy-done.2
  2.1 0.0 copy-done.3
  2.1 0.0 copy-start
  2.1 1.0 copy-done
  3.2 102.3 %shard_map.104 = (f32[8,128,128]{2,1,0:T(8,128)S(1)}, f32[8,128,128]{2,1,0:T(8,128)S(1)}) custom-call(f32[8,128,128]{2,1,0:T(8,128)S(1)} %copy-done, f32[8,128,128]{2,1,0:T(8,128)} %exch_hbm.1, f32[8,128]{1,0:T(8,128)S(1)} %copy-done.1, f32[8]{0:T(128)S(1)} %copy-done.3, bf16[8,512,128]{2,1,0:T(8,128)(2,1)} %coef_ref.1, s32[8,4]{1,0:T(8,128)S(1)} %copy.12.tiles_ref, ...), custom_call_target="tpu_custom_call" | custom-call | tf_op jit(solution)/shard_map/pallas_call | solution.py:499
  105.5 0.8 copy.15
  106.3 0.8 copy.16
  (1 shorter events, 0.0 us)
Async XLA Ops:
  0.6 0.8 copy-start.5
  0.6 0.8 copy-start.4
  1.4 0.7 copy-start.1
  1.4 0.7 copy-start.2
  1.4 0.7 copy-start.3
  2.1 1.0 copy-start

commit v8 on v6

--- a/solution.py
+++ b/solution.py
@@ -313,9 +313,9 @@
 
 def kernel(
     amp_hbm, exch_hbm, energy_ref, shift_ref, coef_ref, tiles_ref, pair_ref, weight_ref,
-    final_ref, residual_ref,
+    current_ref, coupled_ref,
     flipped, straight, coef_all, turned, amp_all, amp_next, high, low, high_t, low_t, up_all, down_all, total,
-    near, near_next, far, far_next, current_all, residual_all, table_out, table_in, table,
+    near, near_next, far, far_next, current_all, coupled_all, table_out, table_in, table,
     amp_own, exch_own,
     own_sem, c_zs, c_zr, c_ys, c_yr, t_zs, t_zr, t_ys, t_yr,
     n_zs, n_zr, n_ys, n_yr, m_zs, m_zr, m_ys, m_yr, peer_send, peer_recv,
@@ -450,25 +450,17 @@
     currents.start()
     levels(late, early, lambda k: couple(at.row(k) * NY, amp_next))
     coupled = Sums(at, total, near_next, far_next, peer_send.at[3], peer_recv.at[3]).run()
-    current = current_all[at.occ]
-    residual_all[at.x, at.core] = exch_own[...] + below * current - coupled
-    residuals = Shares(at, residual_all, peer_send.at[4], peer_recv.at[4])
-    residuals.start()
-
-    @pl.loop(0, PAIRS)
-    def _(p):
-        final_ref[p] = denominator(p)
-
+    coupled_all[at.x, at.core] = coupled
+    sums = Shares(at, coupled_all, peer_send.at[4], peer_recv.at[4])
+    sums.start()
     currents.arrived()
-    residuals.arrived()
-
-    @pl.loop(0, PAIRS)
-    def _(p):
-        residual = residual_all[p // NC, lax.rem(p, NC)]
-        residual_ref[p] = residual
-        final_ref[p] = current_all[p] - residual / final_ref[p]
-
-    for copies in (coefs, amps, tables, late, early, currents, residuals):
+    current_ref[...] = current_all[...]
+    sums.arrived()
+    for x in range(NX):
+        for core in range(NC):
+            coupled_ref[x * NC + core] = coupled_all[x, core]
+
+    for copies in (coefs, amps, tables, late, early, currents, sums):
         copies.sent()
 
 
@@ -496,7 +488,7 @@
     )
     block = (N, N)
     out = jax.ShapeDtypeStruct((PAIRS, N, N), F32)
-    return pl.pallas_call(
+    current, coupled = pl.pallas_call(
         kernel,
         out_shape=(out, out),
         in_specs=[hbm, hbm, vmem, smem, vmem, smem, vmem, vmem],
@@ -538,6 +530,9 @@
         amplitudes, exchange_ints, pno_energy, pair_shift, coefficients, domain_tiles,
         coupled_pair, couple_weight[0],
     )
+    denominator = pno_energy[:, :, None] + pno_energy[:, None, :] + pair_shift[:, None, None]
+    residual = exchange_ints + denominator * current - coupled
+    return current - residual / denominator, residual
 
 
 def solution(mesh):

time: 107 us -> 107 us (level)
  local copies, waits for them, and re-layouts: 4.09 us -> 2.5 us
  other arithmetic: 0.01 us -> 1.2 us
    unnamed x15, local copies, waits for them, and re-layouts: 4.09 us -> 2.5 us
    sub x0 -> x1, other arithmetic: none -> 1.2 us  [local(): return (current - residual / denominator, residual)]
where the time goes in v8:
time: 107 us; the launch traced here: 106 us
  Pallas kernels  102 us (95%)
  local copies, waits for them, and re-layouts  2.5 us (2%)
  other arithmetic  1.2 us (1%)
    pallas_call x1, Pallas kernels, local(): pl.pallas_call(kernel, out_shape=(out, out), in_specs=[hbm, hbm, vmem, sm...  102 us
    unnamed x15, local copies, waits for them, and re-layouts  2.5 us

profile of v8, /device:TPU:1, one launch (start us, length us, event | category | flops | bytes accessed | tf_op | source)
XLA Modules:
  0.0 106.4 jit_solution(6685744221618393989)
XLA Ops:
  0.6 0.0 copy-start.6
  0.6 0.0 copy-start.5
  0.7 0.8 copy.12.tiles_ref
  1.4 0.0 copy-done.6
  1.4 0.0 copy-done.5
  1.4 0.0 copy-start.1
  1.4 0.0 copy-start.2
  1.4 0.0 copy-start.3
  1.5 0.7 copy-done.1
  2.1 0.0 copy-done.2
  2.1 0.0 copy-done.3
  2.1 0.0 copy-start
  2.1 1.0 copy-done
  3.2 0.0 copy-start.4
  3.2 102.0 %shard_map.104 = (f32[8,128,128]{2,1,0:T(8,128)S(1)}, f32[8,128,128]{2,1,0:T(8,128)S(1)}) custom-call(f32[8,128,128]{2,1,0:T(8,128)S(1)} %copy-done, f32[8,128,128]{2,1,0:T(8,128)} %exch_hbm.1, f32[8,128]{1,0:T(8,128)S(1)} %copy-done.1, f32[8]{0:T(128)S(1)} %copy-done.3, bf16[8,512,128]{2,1,0:T(8,128)(2,1)} %coef_ref.1, s32[8,4]{1,0:T(8,128)S(1)} %copy.12.tiles_ref, ...), custom_call_target="tpu_custom_call" | custom-call | tf_op jit(solution)/shard_map/pallas_call | solution.py:491
  105.1 0.0 copy-done.4
  105.2 1.2 %divide_subtract_fusion = (f32[8,128,128]{2,1,0:T(8,128)}, f32[8,128,128]{2,1,0:T(8,128)}) fusion(f32[8,128,128]{2,1,0:T(8,128)S(1)} %get-tuple-element.4, f32[8]{0:T(128)S(1)} %copy-done.3, f32[8,128]{1,0:T(8,128)S(1)} %copy-done.1, f32[8,128,128]{2,1,0:T(8,128)S(1)} %get-tuple-element.5, f32[8,128,128]{2,1,0:T(8,128)S(1)} %copy-done.4), kind=kLoop, calls=%fused_computation | loop fusion | flops 917504 | bytes 2625568 | tf_op jit(solution)/shard_map/sub | solution.py:535
  (1 shorter events, 0.0 us)
Async XLA Ops:
  0.6 0.8 copy-start.6
  0.6 0.8 copy-start.5
  1.4 0.7 copy-start.1
  1.4 0.7 copy-start.2
  1.4 0.7 copy-start.3
  2.1 1.0 copy-start
  3.2 102.0 %copy-start.4 = (f32[8,128,128]{2,1,0:T(8,128)S(1)}, f32[8,128,128]{2,1,0:T(8,128)}, u32[]{:S(2)}) copy-start(f32[8,128,128]{2,1,0:T(8,128)} %exch_hbm.1) | copy-start | bytes 1572868
